TPU v7x, 32 devices: a whole 2x2x4 slice. The times are simulated.
32 devices in a mesh: ctx: 16 (over z, y, core), head: 2 (over x).
Axes of the slice: x: 2, y: 2, z: 4, core: 2. Of those that a mesh axis runs over, the one named last changes fastest.
Arguments:
- queries: bfloat16 [4096, 2048], P('ctx', 'head'), may hold values from -120 to 120
- keys: bfloat16 [4096, 128], P('ctx'), may hold values from -20 to 20
- values: bfloat16 [4096, 128], P('ctx'), may hold values from -6 to 6
- grad_out: bfloat16 [4096, 2048], P('ctx', 'head'), may hold values from -6 to 6
- doc_of_block: int32 [16], replicated, may hold values from 0 to 3, never falling along the last dimension, each value on 1 to 8 neighbouring positions
- pair_list: int32 [16, 7], P('ctx'), may hold values from 0 to 7, as said below
- knock: int32 [16, 16], P('head'), may hold values 0 or 1
Outputs:
- d_queries: bfloat16 [4096, 2048], P('ctx', 'head')
- d_keys: bfloat16 [4096, 128], P('ctx')
- d_values: bfloat16 [4096, 128], P('ctx')
Inputs may be any that keep to these rules, and one draw needn't show every extreme that they name: `pair_list`: row b holds distinct offsets from 1 to 7 in its first entries and 0 in the rest; some row holds all 7 offsets; an offset that reaches before block 0 names no block. `doc_of_block`: never falls along the blocks; each document covers 1 to 8 whole blocks, one exactly 8.
All inputs are finite; a program needn't handle non-finite values. No bound on the sum of `knock` on one device may be relied on, other than what follows from the above.
Results may differ from a plain program's by a relative error of at most 0.01.
Values may be sent and summed in bfloat16 or wider, within the bound.
A program may use at most 128 MiB of HBM per device.

v0:
```python
import jax
import jax.numpy as jnp
from jax import lax
from jax.sharding import PartitionSpec as P

NEG = -1e30


def from_behind(array, axis, by):
    size = lax.axis_size(axis)
    pairs = [(i, i + by) for i in range(size) if 0 <= i + by < size]
    return lax.ppermute(array, axis, pairs)


def local(queries, keys, values, grad_out, doc_of_block, pair_list, knock):
    rows = keys.shape[0]
    width = keys.shape[1]
    local_heads = queries.shape[1] // width
    reach = pair_list.shape[1] + 1
    blocks = doc_of_block.shape[0]
    scale = width ** (-0.5)
    here = lax.axis_index("ctx")
    query_heads = queries.reshape(rows, local_heads, width)
    grad_heads = grad_out.reshape(rows, local_heads, width)
    packed = jnp.concatenate([keys, values], axis=1)
    lower = jnp.arange(rows)[:, None] >= jnp.arange(rows)[None, :]
    own_doc = lax.dynamic_index_in_dim(doc_of_block, here, 0, keepdims=False)

    def tile_mask(offset):
        if offset == 0:
            return jnp.broadcast_to(lower[None], (local_heads, rows, rows))
        source = here - offset
        clipped = jnp.clip(source, 0, blocks - 1)
        listed = jnp.any(pair_list[0] == offset)
        same_doc = lax.dynamic_index_in_dim(doc_of_block, clipped, 0, keepdims=False) == own_doc
        keeping = lax.dynamic_index_in_dim(knock, clipped, 1, keepdims=False) == 1
        allowed = (source >= 0) & listed & same_doc & keeping
        return jnp.broadcast_to(allowed[:, None, None], (local_heads, rows, rows))

    tiles = [packed]
    current = packed
    for offset in range(1, reach):
        current = from_behind(current, "ctx", 1)
        tiles.append(current)
    top = jnp.full((local_heads, rows, 1), NEG, jnp.float32)
    total = jnp.zeros((local_heads, rows, 1), jnp.float32)
    weighted = jnp.zeros((local_heads, rows, 1), jnp.float32)
    kept = []
    masks = []
    for offset in range(reach):
        mask = tile_mask(offset)
        masks.append(mask)
        first_tile = tiles[offset]
        raw = (
            jnp.einsum(
                "ihd,jd->hij",
                query_heads,
                first_tile[:, :width],
                preferred_element_type=jnp.float32,
            )
            * scale
        )
        scores = jnp.where(mask, raw, NEG)
        grad_probs = jnp.einsum(
            "ihd,jd->hij", grad_heads, first_tile[:, width:], preferred_element_type=jnp.float32
        )
        new_top = jnp.maximum(top, jnp.max(scores, axis=2, keepdims=True))
        factor = jnp.exp(top - new_top)
        shifted = jnp.exp(scores - new_top)
        new_total = total * factor + jnp.sum(shifted, axis=2, keepdims=True)
        new_weighted = weighted * factor + jnp.sum(shifted * grad_probs, axis=2, keepdims=True)
        scores, grad_probs, top, total, weighted = (
            scores,
            grad_probs,
            new_top,
            new_total,
            new_weighted,
        )
        kept.append((scores, grad_probs))
    log_total = top + jnp.log(total)
    delta = weighted / total

    def grad_step(tile, scores, grad_probs, query_sum):
        probs = jnp.exp(scores - log_total)
        grad_scores = probs * (grad_probs - delta)
        probs_low = probs.astype(jnp.bfloat16)
        grad_low = grad_scores.astype(jnp.bfloat16)
        query_add = jnp.einsum(
            "hij,jd->ihd", grad_low, tile[:, :width], preferred_element_type=jnp.float32
        )
        key_part = (
            jnp.einsum("hij,ihd->jd", grad_low, query_heads, preferred_element_type=jnp.float32)
            * scale
        )
        value_part = jnp.einsum(
            "hij,ihd->jd", probs_low, grad_heads, preferred_element_type=jnp.float32
        )
        return (query_sum + query_add, jnp.concatenate([key_part, value_part], axis=1))

    def grad_tile(offset, query_sum):
        scores, grad_probs = kept[offset]
        return grad_step(tiles[offset], scores, grad_probs, query_sum)

    query_sum = jnp.zeros((rows, local_heads, width), jnp.float32)
    carried = None
    for offset in reversed(range(reach)):
        query_sum, term = grad_tile(offset, query_sum)
        if carried is None:
            carried = term
        else:
            carried = (
                from_behind(carried.astype(jnp.bfloat16), "ctx", -1).astype(carried.dtype) + term
            )
    result = lax.psum(carried, "head").astype(jnp.bfloat16)
    d_queries = (query_sum * scale).reshape(rows, local_heads * width).astype(jnp.bfloat16)
    return (d_queries, result[:, :width], result[:, width:])


def solution(mesh):
    in_specs = (
        P("ctx", "head"),
        P("ctx", None),
        P("ctx", None),
        P("ctx", "head"),
        P(),
        P("ctx", None),
        P("head", None),
    )
    out_specs = (P("ctx", "head"), P("ctx", None), P("ctx", None))
    return jax.shard_map(local, mesh=mesh, in_specs=in_specs, out_specs=out_specs, check_vma=False)
```

profile of v0, /device:TPU:21, one launch (start us, length us, event | category | flops | bytes accessed | tf_op | source)
XLA Modules:
  0.0 170.0 jit_solution(16317927705270088234)
XLA Ops:
  0.6 0.9 pad_maximum_fusion
  1.5 3.7 %collective-permute-start = (bf16[256,256]{1,0:T(8,128)(2,1)S(1)}, bf16[256,256]{1,0:T(8,128)(2,1)S(1)}, u32[]{:S(2)}, u32[]{:S(2)}) collective-permute-start(bf16[256,256]{1,0:T(8,128)(2,1)S(1)} %pad_maximum_fusion), channel_id=1, source_target_pairs={{0,2},{2,4},{4,6},{6,8},{8,10},{10,12},{12,14},{14,16},{16,18},{18... | collective-permute-start | bytes 393224 | tf_op jit(solution)/shard_map/ppermute | solution.py:12
  5.3 1.2 copy.117
  6.6 1.3 fusion.131
  7.9 0.7 fusion.130
  16.9 1.2 copy.118
  18.2 0.8 compare_reduce_fusion
  23.7 1.9 %collective-permute-start.1 = (bf16[256,256]{1,0:T(8,128)(2,1)S(1)}, bf16[256,256]{1,0:T(8,128)(2,1)S(1)}, u32[]{:S(2)}, u32[]{:S(2)}) collective-permute-start(bf16[256,256]{1,0:T(8,128)(2,1)S(1)} %collective-permute-done), channel_id=1, source_target_pairs={{0,2},{2,4},{4,6},{6,8},{8,10},{10,12},{12,14},{14,16},{16,18},{18... | collective-permute-start | bytes 393224 | tf_op jit(solution)/shard_map/ppermute | solution.py:12
  26.1 1.5 collective-permute-done.1
  27.6 5.2 %collective-permute-start.2 = (bf16[256,256]{1,0:T(8,128)(2,1)S(1)}, bf16[256,256]{1,0:T(8,128)(2,1)S(1)}, u32[]{:S(2)}, u32[]{:S(2)}) collective-permute-start(bf16[256,256]{1,0:T(8,128)(2,1)S(1)} %collective-permute-done.1), channel_id=1, source_target_pairs={{0,2},{2,4},{4,6},{6,8},{8,10},{10,12},{12,14},{14,16},{16,18},{18... | collective-permute-start | bytes 393224 | tf_op jit(solution)/shard_map/ppermute | solution.py:12
  33.3 1.5 collective-permute-done.2
  34.7 5.2 %collective-permute-start.3 = (bf16[256,256]{1,0:T(8,128)(2,1)S(1)}, bf16[256,256]{1,0:T(8,128)(2,1)S(1)}, u32[]{:S(2)}, u32[]{:S(2)}) collective-permute-start(bf16[256,256]{1,0:T(8,128)(2,1)S(1)} %collective-permute-done.2), channel_id=1, source_target_pairs={{0,2},{2,4},{4,6},{6,8},{8,10},{10,12},{12,14},{14,16},{16,18},{18... | collective-permute-start | bytes 393224 | tf_op jit(solution)/shard_map/ppermute | solution.py:12
  40.4 1.5 collective-permute-done.3
  41.9 5.2 %collective-permute-start.4 = (bf16[256,256]{1,0:T(8,128)(2,1)S(1)}, bf16[256,256]{1,0:T(8,128)(2,1)S(1)}, u32[]{:S(2)}, u32[]{:S(2)}) collective-permute-start(bf16[256,256]{1,0:T(8,128)(2,1)S(1)} %collective-permute-done.3), channel_id=1, source_target_pairs={{0,2},{2,4},{4,6},{6,8},{8,10},{10,12},{12,14},{14,16},{16,18},{18... | collective-permute-start | bytes 393224 | tf_op jit(solution)/shard_map/ppermute | solution.py:12
  47.6 1.5 collective-permute-done.4
  49.1 5.2 %collective-permute-start.5 = (bf16[256,256]{1,0:T(8,128)(2,1)S(1)}, bf16[256,256]{1,0:T(8,128)(2,1)S(1)}, u32[]{:S(2)}, u32[]{:S(2)}) collective-permute-start(bf16[256,256]{1,0:T(8,128)(2,1)S(1)} %collective-permute-done.4), channel_id=1, source_target_pairs={{0,2},{2,4},{4,6},{6,8},{8,10},{10,12},{12,14},{14,16},{16,18},{18... | collective-permute-start | bytes 393224 | tf_op jit(solution)/shard_map/ppermute | solution.py:12
  54.8 1.5 collective-permute-done.5
  56.3 5.4 %collective-permute-start.6 = (bf16[256,256]{1,0:T(8,128)(2,1)S(1)}, bf16[256,256]{1,0:T(8,128)(2,1)S(1)}, u32[]{:S(2)}, u32[]{:S(2)}) collective-permute-start(bf16[256,256]{1,0:T(8,128)(2,1)S(1)} %collective-permute-done.5), channel_id=1, source_target_pairs={{0,2},{2,4},{4,6},{6,8},{8,10},{10,12},{12,14},{14,16},{16,18},{18... | collective-permute-start | bytes 393224 | tf_op jit(solution)/shard_map/ppermute | solution.py:12
  62.2 1.3 collective-permute-done.6
  63.9 2.0 %fusion.18 = (f32[8,256]{1,0:T(8,128)S(1)}, f32[8,256]{1,0:T(8,128)S(1)}, f32[256,256,8]{1,0,2:T(8,128)}) fusion(f32[8,256,256]{1,2,0:T(8,128)S(1)} %get-tuple-element.79, f32[8,256]{1,0:T(8,128)S(1)} %get-tuple-element.55, bf16[256,8,128]{0,2,1:T(8,128)(2,1)S(1)} %bitcast.426, bf16[256,128]{1,0:T(8,128)(2,1)S(1)} %copy-done.38), kind=kOutput, calls=%fused_computation.32 | convolution fusion | flops 136310784 | bytes 4808704 | tf_op jit(solution)/shard_map/ihd,jd->hij/dot_general | solution.py:64
  65.9 1.8 %fusion.21 = (f32[8,256]{1,0:T(8,128)S(1)}, f32[8,256]{1,0:T(8,128)S(1)}, f32[256,256,8]{1,0,2:T(8,128)}) fusion(f32[256,256,8]{1,0,2:T(8,128)S(1)} %get-tuple-element.65, f32[8,256]{1,0:T(8,128)S(1)} %get-tuple-element.38, bf16[256,8,128]{0,2,1:T(8,128)(2,1)S(1)} %bitcast.427, bf16[256,256]{1,0:T(8,128)(2,1)S(1)} %collective-permute-done.6), kind=kOutput, calls=%fused_computation.37 | convolution fusion | flops 136310784 | bytes 4808704 | tf_op jit(solution)/shard_map/ihd,jd->hij/dot_general | solution.py:64
  67.8 1.8 %fusion = (f32[8,256]{1,0:T(8,128)S(1)}, f32[8,256]{1,0:T(8,128)S(1)}, f32[256,256,8]{1,0,2:T(8,128)}) fusion(f32[256,256,8]{1,0,2:T(8,128)S(1)} %get-tuple-element.67, f32[8,256]{1,0:T(8,128)S(1)} %get-tuple-element.39, bf16[256,8,128]{0,2,1:T(8,128)(2,1)S(1)} %bitcast.428, bf16[256,256]{1,0:T(8,128)(2,1)S(1)} %collective-permute-done.5), kind=kOutput, calls=%fused_computation.2 | convolution fusion | flops 136310784 | bytes 4808704 | tf_op jit(solution)/shard_map/ihd,jd->hij/dot_general | solution.py:64
  69.6 1.8 %fusion.3 = (f32[8,256]{1,0:T(8,128)S(1)}, f32[8,256]{1,0:T(8,128)S(1)}, f32[256,256,8]{1,0,2:T(8,128)}) fusion(f32[256,256,8]{1,0,2:T(8,128)S(1)} %get-tuple-element.69, f32[8,256]{1,0:T(8,128)S(1)} %get-tuple-element.40, bf16[256,8,128]{0,2,1:T(8,128)(2,1)S(1)} %bitcast.429, bf16[256,256]{1,0:T(8,128)(2,1)S(1)} %collective-permute-done.4), kind=kOutput, calls=%fused_computation.7 | convolution fusion | flops 136310784 | bytes 4808704 | tf_op jit(solution)/shard_map/ihd,jd->hij/dot_general | solution.py:64
  71.3 1.8 %fusion.6 = (f32[8,256]{1,0:T(8,128)S(1)}, f32[8,256]{1,0:T(8,128)S(1)}, f32[256,256,8]{1,0,2:T(8,128)}) fusion(f32[256,256,8]{1,0,2:T(8,128)S(1)} %get-tuple-element.71, f32[8,256]{1,0:T(8,128)S(1)} %get-tuple-element.41, bf16[256,8,128]{0,2,1:T(8,128)(2,1)S(1)} %bitcast.430, bf16[256,256]{1,0:T(8,128)(2,1)S(1)} %collective-permute-done.3), kind=kOutput, calls=%fused_computation.12 | convolution fusion | flops 136310784 | bytes 4808704 | tf_op jit(solution)/shard_map/ihd,jd->hij/dot_general | solution.py:64
  73.1 1.8 %fusion.9 = (f32[8,256]{1,0:T(8,128)S(1)}, f32[8,256]{1,0:T(8,128)S(1)}, f32[256,256,8]{1,0,2:T(8,128)}) fusion(f32[256,256,8]{1,0,2:T(8,128)S(1)} %get-tuple-element.73, f32[8,256]{1,0:T(8,128)S(1)} %get-tuple-element.42, bf16[256,8,128]{0,2,1:T(8,128)(2,1)S(1)} %bitcast.431, bf16[256,256]{1,0:T(8,128)(2,1)S(1)} %collective-permute-done.2), kind=kOutput, calls=%fused_computation.17 | convolution fusion | flops 136310784 | bytes 4808704 | tf_op jit(solution)/shard_map/ihd,jd->hij/dot_general | solution.py:64
  75.0 1.9 %fusion.12 = (f32[8,256]{1,0:T(8,128)S(1)}, f32[8,256]{1,0:T(8,128)S(1)}, f32[256,256,8]{1,0,2:T(8,128)}) fusion(f32[256,256,8]{1,0,2:T(8,128)S(1)} %get-tuple-element.75, f32[8,256]{1,0:T(8,128)S(1)} %get-tuple-element.43, bf16[256,8,128]{0,2,1:T(8,128)(2,1)S(1)} %bitcast.432, bf16[256,256]{1,0:T(8,128)(2,1)S(1)} %collective-permute-done.1), kind=kOutput, calls=%fused_computation.22 | convolution fusion | flops 136310784 | bytes 4808704 | tf_op jit(solution)/shard_map/ihd,jd->hij/dot_general | solution.py:64
  76.8 1.8 %fusion.15 = (f32[8,256]{1,0:T(8,128)S(1)}, f32[8,256]{1,0:T(8,128)S(1)}, f32[256,256,8]{1,0,2:T(8,128)}) fusion(f32[256,256,8]{1,0,2:T(8,128)S(1)} %get-tuple-element.77, f32[8,256]{1,0:T(8,128)S(1)} %get-tuple-element.44, bf16[256,8,128]{0,2,1:T(8,128)(2,1)S(1)} %bitcast.433, bf16[256,256]{1,0:T(8,128)(2,1)S(1)} %collective-permute-done), kind=kOutput, calls=%fused_computation.27 | convolution fusion | flops 136310784 | bytes 4808704 | tf_op jit(solution)/shard_map/ihd,jd->hij/dot_general | solution.py:64
  78.6 1.1 fusion.71
  79.8 12.2 %fusion.23 = (bf16[8,256,256]{1,2,0:T(8,128)(2,1)S(1)}, bf16[8,256,256]{1,2,0:T(8,128)(2,1)}, bf16[8,256,256]{1,2,0:T(8,128)(2,1)}, bf16[8,256,256]{1,2,0:T(8,12...) fusion(f32[256,256,8]{1,0,2:T(8,128)} %get-tuple-element.80, ...), kind=kLoop, calls=%fused_computation.39 | loop fusion | flops 16777216 | bytes 41959424 | tf_op jit(solution)/shard_map/convert_element_type | solution.py:87
  92.1 1.8 %fusion.63 = f32[256,128]{0,1:T(8,128)S(1)} fusion(bf16[8,256,256]{1,2,0:T(8,128)(2,1)} %get-tuple-element.54, bf16[256,8,128]{0,2,1:T(8,128)(2,1)S(1)} %bitcast.418), kind=kOutput, calls=%fused_computation.114 | convolution fusion | flops 134250496 | bytes 1703936 | tf_op jit(solution)/shard_map/hij,ihd->jd/dot_general | solution.py:92
  94.2 1.1 fusion.72
  95.4 1.1 fusion.69
  96.5 1.1 fusion.68
  97.6 1.1 fusion.67
  98.8 1.1 fusion.66
  99.9 0.5 fusion.65
  100.4 0.5 fusion.64
  103.6 0.6 fusion.62
  104.2 1.0 copy.74
  105.2 1.0 pad_maximum_fusion.1
  106.3 2.1 %collective-permute-start.7 = (bf16[256,256]{0,1:T(8,128)(2,1)S(1)}, bf16[256,256]{0,1:T(8,128)(2,1)S(1)}, u32[]{:S(2)}, u32[]{:S(2)}) collective-permute-start(bf16[256,256]{0,1:T(8,128)(2,1)S(1)} %pad_maximum_fusion.1), channel_id=1, source_target_pairs={{2,0},{4,2},{6,4},{8,6},{10,8},{12,10},{14,12},{16,14},{18,16},{20... | collective-permute-start | bytes 393224 | tf_op jit(solution)/shard_map/ppermute | solution.py:12
  108.4 2.1 %convolution_bitcast_fusion.13 = f32[256,128]{0,1:T(8,128)S(1)} fusion(bf16[256,8,128]{0,2,1:T(8,128)(2,1)S(1)} %bitcast.435, f32[256,256,8]{1,0,2:T(8,128)} %copy-done.10, f32[8,256]{1,0:T(8,128)S(1)} %get-tuple-element.36), kind=kOutput, calls=%fused_computation.130 | convolution fusion | flops 135266304 | bytes 2760704 | tf_op jit(solution)/shard_map/hij,ihd->jd/dot_general | solution.py:95
  110.5 3.6 %collective-permute-done.7 = bf16[256,256]{0,1:T(8,128)(2,1)S(1)} collective-permute-done((bf16[256,256]{0,1:T(8,128)(2,1)S(1)}, bf16[256,256]{0,1:T(8,128)(2,1)S(1)}, u32[]{:S(2)}, u32[]{:S(2)}) %collective-permute-start.7) | collective-permute-done | bytes 131104 | tf_op jit(solution)/shard_map/ppermute | solution.py:12
  114.2 1.9 %collective-permute-start.8 = (bf16[256,256]{0,1:T(8,128)(2,1)S(1)}, bf16[256,256]{0,1:T(8,128)(2,1)S(1)}, u32[]{:S(2)}, u32[]{:S(2)}) collective-permute-start(bf16[256,256]{0,1:T(8,128)(2,1)S(1)} %fusion.89), channel_id=1, source_target_pairs={{2,0},{4,2},{6,4},{8,6},{10,8},{12,10},{14,12},{16,14},{18,16},{20... | collective-permute-start | bytes 393224 | tf_op jit(solution)/shard_map/ppermute | solution.py:12
  116.1 0.5 convolution_bitcast_fusion.11
  116.7 4.7 %collective-permute-done.8 = bf16[256,256]{0,1:T(8,128)(2,1)S(1)} collective-permute-done((bf16[256,256]{0,1:T(8,128)(2,1)S(1)}, bf16[256,256]{0,1:T(8,128)(2,1)S(1)}, u32[]{:S(2)}, u32[]{:S(2)}) %collective-permute-start.8) | collective-permute-done | bytes 131104 | tf_op jit(solution)/shard_map/ppermute | solution.py:12
  121.4 1.9 %collective-permute-start.9 = (bf16[256,256]{0,1:T(8,128)(2,1)S(1)}, bf16[256,256]{0,1:T(8,128)(2,1)S(1)}, u32[]{:S(2)}, u32[]{:S(2)}) collective-permute-start(bf16[256,256]{0,1:T(8,128)(2,1)S(1)} %fusion.90), channel_id=1, source_target_pairs={{2,0},{4,2},{6,4},{8,6},{10,8},{12,10},{14,12},{16,14},{18,16},{20... | collective-permute-start | bytes 393224 | tf_op jit(solution)/shard_map/ppermute | solution.py:12
  123.4 0.5 convolution_bitcast_fusion.9
  123.9 4.7 %collective-permute-done.9 = bf16[256,256]{0,1:T(8,128)(2,1)S(1)} collective-permute-done((bf16[256,256]{0,1:T(8,128)(2,1)S(1)}, bf16[256,256]{0,1:T(8,128)(2,1)S(1)}, u32[]{:S(2)}, u32[]{:S(2)}) %collective-permute-start.9) | collective-permute-done | bytes 131104 | tf_op jit(solution)/shard_map/ppermute | solution.py:12
  128.6 1.9 %collective-permute-start.10 = (bf16[256,256]{0,1:T(8,128)(2,1)S(1)}, bf16[256,256]{0,1:T(8,128)(2,1)S(1)}, u32[]{:S(2)}, u32[]{:S(2)}) collective-permute-start(bf16[256,256]{0,1:T(8,128)(2,1)S(1)} %fusion.91), channel_id=1, source_target_pairs={{2,0},{4,2},{6,4},{8,6},{10,8},{12,10},{14,12},{16,14},{18,16},{20... | collective-permute-start | bytes 393224 | tf_op jit(solution)/shard_map/ppermute | solution.py:12
  130.6 0.5 convolution_bitcast_fusion.7
  131.1 4.7 %collective-permute-done.10 = bf16[256,256]{0,1:T(8,128)(2,1)S(1)} collective-permute-done((bf16[256,256]{0,1:T(8,128)(2,1)S(1)}, bf16[256,256]{0,1:T(8,128)(2,1)S(1)}, u32[]{:S(2)}, u32[]{:S(2)}) %collective-permute-start.10) | collective-permute-done | bytes 131104 | tf_op jit(solution)/shard_map/ppermute | solution.py:12
  135.9 1.9 %collective-permute-start.11 = (bf16[256,256]{0,1:T(8,128)(2,1)S(1)}, bf16[256,256]{0,1:T(8,128)(2,1)S(1)}, u32[]{:S(2)}, u32[]{:S(2)}) collective-permute-start(bf16[256,256]{0,1:T(8,128)(2,1)S(1)} %fusion.92), channel_id=1, source_target_pairs={{2,0},{4,2},{6,4},{8,6},{10,8},{12,10},{14,12},{16,14},{18,16},{20... | collective-permute-start | bytes 393224 | tf_op jit(solution)/shard_map/ppermute | solution.py:12
  137.8 0.5 convolution_bitcast_fusion.5
  138.3 4.7 %collective-permute-done.11 = bf16[256,256]{0,1:T(8,128)(2,1)S(1)} collective-permute-done((bf16[256,256]{0,1:T(8,128)(2,1)S(1)}, bf16[256,256]{0,1:T(8,128)(2,1)S(1)}, u32[]{:S(2)}, u32[]{:S(2)}) %collective-permute-start.11) | collective-permute-done | bytes 131104 | tf_op jit(solution)/shard_map/ppermute | solution.py:12
  143.1 1.9 %collective-permute-start.12 = (bf16[256,256]{0,1:T(8,128)(2,1)S(1)}, bf16[256,256]{0,1:T(8,128)(2,1)S(1)}, u32[]{:S(2)}, u32[]{:S(2)}) collective-permute-start(bf16[256,256]{0,1:T(8,128)(2,1)S(1)} %fusion.93), channel_id=1, source_target_pairs={{2,0},{4,2},{6,4},{8,6},{10,8},{12,10},{14,12},{16,14},{18,16},{20... | collective-permute-start | bytes 393224 | tf_op jit(solution)/shard_map/ppermute | solution.py:12
  145.0 0.5 convolution_bitcast_fusion.3
  145.5 4.7 %collective-permute-done.12 = bf16[256,256]{0,1:T(8,128)(2,1)S(1)} collective-permute-done((bf16[256,256]{0,1:T(8,128)(2,1)S(1)}, bf16[256,256]{0,1:T(8,128)(2,1)S(1)}, u32[]{:S(2)}, u32[]{:S(2)}) %collective-permute-start.12) | collective-permute-done | bytes 131104 | tf_op jit(solution)/shard_map/ppermute | solution.py:12
  150.3 1.9 %collective-permute-start.13 = (bf16[256,256]{0,1:T(8,128)(2,1)S(1)}, bf16[256,256]{0,1:T(8,128)(2,1)S(1)}, u32[]{:S(2)}, u32[]{:S(2)}) collective-permute-start(bf16[256,256]{0,1:T(8,128)(2,1)S(1)} %fusion.94), channel_id=1, source_target_pairs={{2,0},{4,2},{6,4},{8,6},{10,8},{12,10},{14,12},{16,14},{18,16},{20... | collective-permute-start | bytes 393224 | tf_op jit(solution)/shard_map/ppermute | solution.py:12
  152.2 0.5 convolution_bitcast_fusion.1
  152.7 4.8 %collective-permute-done.13 = bf16[256,256]{0,1:T(8,128)(2,1)S(1)} collective-permute-done((bf16[256,256]{0,1:T(8,128)(2,1)S(1)}, bf16[256,256]{0,1:T(8,128)(2,1)S(1)}, u32[]{:S(2)}, u32[]{:S(2)}) %collective-permute-start.13) | collective-permute-done | bytes 131104 | tf_op jit(solution)/shard_map/ppermute | solution.py:12
  157.5 11.0 %all-reduce.1 = bf16[256,256]{0,1:T(8,128)(2,1)S(1)} all-reduce(f32[256,256]{0,1:T(8,128)S(1)} %maximum_add_fusion.6), channel_id=1, replica_groups=mesh['ctx'=16,'head'=2] {'head'}, use_global_device_ids=true, to_apply=%region_31.32 | all-reduce | flops 65536 | bytes 393216 | tf_op jit(solution)/shard_map/psum | solution.py:114
  168.5 0.7 copy.76
  169.2 0.7 copy.75
  (112 shorter events, 6.9 us)
Async XLA Ops:
  0.6 7.3 %copy-start.40 = (s32[16]{0:T(128)S(1)}, s32[16]{0:T(128)}, u32[]{:S(2)}) copy-start(s32[16]{0:T(128)} %param.11) | copy-start | bytes 196
  1.5 22.2 %collective-permute-start = (bf16[256,256]{1,0:T(8,128)(2,1)S(1)}, bf16[256,256]{1,0:T(8,128)(2,1)S(1)}, u32[]{:S(2)}, u32[]{:S(2)}) collective-permute-start(bf16[256,256]{1,0:T(8,128)(2,1)S(1)} %pad_maximum_fusion), channel_id=1, source_target_pairs={{0,2},{2,4},{4,6},{6,8},{8,10},{10,12},{12,14},{14,16},{16,18},{18... | collective-permute-start | bytes 393224 | tf_op jit(solution)/shard_map/ppermute | solution.py:12
  6.5 11.6 %copy-start.41 = (s32[1,7]{1,0:T(1,128)S(1)}, s32[1,7]{1,0:T(1,128)}, u32[]{:S(2)}) copy-start(s32[1,7]{1,0:T(1,128)} %param.12) | copy-start | bytes 88
  6.5 16.8 %copy-start.39 = (s32[8,16]{1,0:T(8,128)S(1)}, s32[8,16]{1,0:T(8,128)}, u32[]{:S(2)}) copy-start(s32[8,16]{1,0:T(8,128)} %param.13) | copy-start | bytes 1540
  23.7 53.1 %copy-start.26 = (bf16[256,256]{1,0:T(8,128)(2,1)}, bf16[256,256]{1,0:T(8,128)(2,1)S(1)}, u32[]{:S(2)}) copy-start(bf16[256,256]{1,0:T(8,128)(2,1)S(1)} %collective-permute-done) | copy-start | bytes 393220
  23.7 3.9 %collective-permute-start.1 = (bf16[256,256]{1,0:T(8,128)(2,1)S(1)}, bf16[256,256]{1,0:T(8,128)(2,1)S(1)}, u32[]{:S(2)}, u32[]{:S(2)}) collective-permute-start(bf16[256,256]{1,0:T(8,128)(2,1)S(1)} %collective-permute-done), channel_id=1, source_target_pairs={{0,2},{2,4},{4,6},{6,8},{8,10},{10,12},{12,14},{14,16},{16,18},{18... | collective-permute-start | bytes 393224 | tf_op jit(solution)/shard_map/ppermute | solution.py:12
  26.1 53.7 %copy-start = (f32[256,256,8]{1,0,2:T(8,128)}, f32[256,256,8]{1,0,2:T(8,128)S(1)}, u32[]{:S(2)}) copy-start(f32[256,256,8]{1,0,2:T(8,128)S(1)} %get-tuple-element.77) | copy-start | bytes 6291460
  27.6 47.4 %copy-start.28 = (bf16[256,256]{1,0:T(8,128)(2,1)}, bf16[256,256]{1,0:T(8,128)(2,1)S(1)}, u32[]{:S(2)}) copy-start(bf16[256,256]{1,0:T(8,128)(2,1)S(1)} %collective-permute-done.1) | copy-start | bytes 393220
  27.6 7.2 %collective-permute-start.2 = (bf16[256,256]{1,0:T(8,128)(2,1)S(1)}, bf16[256,256]{1,0:T(8,128)(2,1)S(1)}, u32[]{:S(2)}, u32[]{:S(2)}) collective-permute-start(bf16[256,256]{1,0:T(8,128)(2,1)S(1)} %collective-permute-done.1), channel_id=1, source_target_pairs={{0,2},{2,4},{4,6},{6,8},{8,10},{10,12},{12,14},{14,16},{16,18},{18... | collective-permute-start | bytes 393224 | tf_op jit(solution)/shard_map/ppermute | solution.py:12
  33.3 46.5 %copy-start.2 = (f32[256,256,8]{1,0,2:T(8,128)}, f32[256,256,8]{1,0,2:T(8,128)S(1)}, u32[]{:S(2)}) copy-start(f32[256,256,8]{1,0,2:T(8,128)S(1)} %get-tuple-element.75) | copy-start | bytes 6291460
  34.7 38.4 %copy-start.30 = (bf16[256,256]{1,0:T(8,128)(2,1)}, bf16[256,256]{1,0:T(8,128)(2,1)S(1)}, u32[]{:S(2)}) copy-start(bf16[256,256]{1,0:T(8,128)(2,1)S(1)} %collective-permute-done.2) | copy-start | bytes 393220
  34.7 7.2 %collective-permute-start.3 = (bf16[256,256]{1,0:T(8,128)(2,1)S(1)}, bf16[256,256]{1,0:T(8,128)(2,1)S(1)}, u32[]{:S(2)}, u32[]{:S(2)}) collective-permute-start(bf16[256,256]{1,0:T(8,128)(2,1)S(1)} %collective-permute-done.2), channel_id=1, source_target_pairs={{0,2},{2,4},{4,6},{6,8},{8,10},{10,12},{12,14},{14,16},{16,18},{18... | collective-permute-start | bytes 393224 | tf_op jit(solution)/shard_map/ppermute | solution.py:12
  40.4 39.4 %copy-start.4 = (f32[256,256,8]{1,0,2:T(8,128)}, f32[256,256,8]{1,0,2:T(8,128)S(1)}, u32[]{:S(2)}) copy-start(f32[256,256,8]{1,0,2:T(8,128)S(1)} %get-tuple-element.73) | copy-start | bytes 6291460
  41.9 29.4 %copy-start.32 = (bf16[256,256]{1,0:T(8,128)(2,1)}, bf16[256,256]{1,0:T(8,128)(2,1)S(1)}, u32[]{:S(2)}) copy-start(bf16[256,256]{1,0:T(8,128)(2,1)S(1)} %collective-permute-done.3) | copy-start | bytes 393220
  41.9 7.2 %collective-permute-start.4 = (bf16[256,256]{1,0:T(8,128)(2,1)S(1)}, bf16[256,256]{1,0:T(8,128)(2,1)S(1)}, u32[]{:S(2)}, u32[]{:S(2)}) collective-permute-start(bf16[256,256]{1,0:T(8,128)(2,1)S(1)} %collective-permute-done.3), channel_id=1, source_target_pairs={{0,2},{2,4},{4,6},{6,8},{8,10},{10,12},{12,14},{14,16},{16,18},{18... | collective-permute-start | bytes 393224 | tf_op jit(solution)/shard_map/ppermute | solution.py:12
  47.6 32.2 %copy-start.6 = (f32[256,256,8]{1,0,2:T(8,128)}, f32[256,256,8]{1,0,2:T(8,128)S(1)}, u32[]{:S(2)}) copy-start(f32[256,256,8]{1,0,2:T(8,128)S(1)} %get-tuple-element.71) | copy-start | bytes 6291460
  49.1 20.5 %copy-start.34 = (bf16[256,256]{1,0:T(8,128)(2,1)}, bf16[256,256]{1,0:T(8,128)(2,1)S(1)}, u32[]{:S(2)}) copy-start(bf16[256,256]{1,0:T(8,128)(2,1)S(1)} %collective-permute-done.4) | copy-start | bytes 393220
  49.1 7.2 %collective-permute-start.5 = (bf16[256,256]{1,0:T(8,128)(2,1)S(1)}, bf16[256,256]{1,0:T(8,128)(2,1)S(1)}, u32[]{:S(2)}, u32[]{:S(2)}) collective-permute-start(bf16[256,256]{1,0:T(8,128)(2,1)S(1)} %collective-permute-done.4), channel_id=1, source_target_pairs={{0,2},{2,4},{4,6},{6,8},{8,10},{10,12},{12,14},{14,16},{16,18},{18... | collective-permute-start | bytes 393224 | tf_op jit(solution)/shard_map/ppermute | solution.py:12
  54.8 14.8 %copy-start.8 = (f32[256,256,8]{1,0,2:T(8,128)}, f32[256,256,8]{1,0,2:T(8,128)S(1)}, u32[]{:S(2)}) copy-start(f32[256,256,8]{1,0,2:T(8,128)S(1)} %get-tuple-element.69) | copy-start | bytes 6291460
  56.3 11.5 %copy-start.36 = (bf16[256,256]{1,0:T(8,128)(2,1)}, bf16[256,256]{1,0:T(8,128)(2,1)S(1)}, u32[]{:S(2)}) copy-start(bf16[256,256]{1,0:T(8,128)(2,1)S(1)} %collective-permute-done.5) | copy-start | bytes 393220
  56.3 7.2 %collective-permute-start.6 = (bf16[256,256]{1,0:T(8,128)(2,1)S(1)}, bf16[256,256]{1,0:T(8,128)(2,1)S(1)}, u32[]{:S(2)}, u32[]{:S(2)}) collective-permute-start(bf16[256,256]{1,0:T(8,128)(2,1)S(1)} %collective-permute-done.5), channel_id=1, source_target_pairs={{0,2},{2,4},{4,6},{6,8},{8,10},{10,12},{12,14},{14,16},{16,18},{18... | collective-permute-start | bytes 393224 | tf_op jit(solution)/shard_map/ppermute | solution.py:12
  62.1 5.6 %copy-start.10 = (f32[256,256,8]{1,0,2:T(8,128)}, f32[256,256,8]{1,0,2:T(8,128)S(1)}, u32[]{:S(2)}) copy-start(f32[256,256,8]{1,0,2:T(8,128)S(1)} %get-tuple-element.67) | copy-start | bytes 6291460
  62.2 1.8 %copy-start.38 = (bf16[256,128]{1,0:T(8,128)(2,1)S(1)}, bf16[256,128]{1,0:T(8,128)(2,1)}, u32[]{:S(2)}) copy-start(bf16[256,128]{1,0:T(8,128)(2,1)} %param.9) | copy-start | bytes 196612
  63.4 2.5 %copy-start.24 = (bf16[256,256]{1,0:T(8,128)(2,1)}, bf16[256,256]{1,0:T(8,128)(2,1)S(1)}, u32[]{:S(2)}) copy-start(bf16[256,256]{1,0:T(8,128)(2,1)S(1)} %collective-permute-done.6) | copy-start | bytes 393220
  63.9 14.7 %copy-start.11 = (f32[256,256,8]{1,0,2:T(8,128)}, f32[256,256,8]{1,0,2:T(8,128)S(1)}, u32[]{:S(2)}) copy-start(f32[256,256,8]{1,0,2:T(8,128)S(1)} %get-tuple-element.65) | copy-start | bytes 6291460
  79.8 14.0 %copy-start.19 = (bf16[256,128]{1,0:T(8,128)(2,1)S(1)}, bf16[256,128]{1,0:T(8,128)(2,1)}, u32[]{:S(2)}) copy-start(bf16[256,128]{1,0:T(8,128)(2,1)} %param.8) | copy-start | bytes 196612
  92.0 1.8 %copy-start.18 = (bf16[8,256,256]{1,2,0:T(8,128)(2,1)S(1)}, bf16[8,256,256]{1,2,0:T(8,128)(2,1)}, u32[]{:S(2)}) copy-start(bf16[8,256,256]{1,2,0:T(8,128)(2,1)} %get-tuple-element.54) | copy-start | bytes 3145732
  93.9 1.5 copy-start.17
  94.2 2.3 %copy-start.16 = (bf16[8,256,256]{1,2,0:T(8,128)(2,1)S(1)}, bf16[8,256,256]{1,2,0:T(8,128)(2,1)}, u32[]{:S(2)}) copy-start(bf16[8,256,256]{1,2,0:T(8,128)(2,1)} %get-tuple-element.49) | copy-start | bytes 3145732
  95.4 2.3 %copy-start.15 = (bf16[8,256,256]{1,2,0:T(8,128)(2,1)S(1)}, bf16[8,256,256]{1,2,0:T(8,128)(2,1)}, u32[]{:S(2)}) copy-start(bf16[8,256,256]{1,2,0:T(8,128)(2,1)} %get-tuple-element.50) | copy-start | bytes 3145732
  96.5 2.3 %copy-start.14 = (bf16[8,256,256]{1,2,0:T(8,128)(2,1)S(1)}, bf16[8,256,256]{1,2,0:T(8,128)(2,1)}, u32[]{:S(2)}) copy-start(bf16[8,256,256]{1,2,0:T(8,128)(2,1)} %get-tuple-element.51) | copy-start | bytes 3145732
  97.6 2.3 %copy-start.13 = (bf16[8,256,256]{1,2,0:T(8,128)(2,1)S(1)}, bf16[8,256,256]{1,2,0:T(8,128)(2,1)}, u32[]{:S(2)}) copy-start(bf16[8,256,256]{1,2,0:T(8,128)(2,1)} %get-tuple-element.52) | copy-start | bytes 3145732
  98.8 1.6 copy-start.12
  99.9 1.0 copy-start.37
  100.4 0.9 copy-start.35
  100.9 0.9 copy-start.33
  101.3 0.9 copy-start.31
  101.8 0.9 copy-start.29
  102.2 0.9 copy-start.27
  102.7 0.9 copy-start.25
  105.2 8.9 %copy-start.23 = (f32[256,128]{0,1:T(8,128)S(1)}, f32[256,128]{0,1:T(8,128)}, u32[]{:S(2)}) copy-start(f32[256,128]{0,1:T(8,128)} %fusion.69) | copy-start | bytes 393220
  105.2 10.9 %copy-start.9 = (f32[256,256,8]{1,0,2:T(8,128)S(1)}, f32[256,256,8]{1,0,2:T(8,128)}, u32[]{:S(2)}) copy-start(f32[256,256,8]{1,0,2:T(8,128)} %copy-done.8) | copy-start | bytes 6291460
  106.3 7.9 %collective-permute-start.7 = (bf16[256,256]{0,1:T(8,128)(2,1)S(1)}, bf16[256,256]{0,1:T(8,128)(2,1)S(1)}, u32[]{:S(2)}, u32[]{:S(2)}) collective-permute-start(bf16[256,256]{0,1:T(8,128)(2,1)S(1)} %pad_maximum_fusion.1), channel_id=1, source_target_pairs={{2,0},{4,2},{6,4},{8,6},{10,8},{12,10},{14,12},{16,14},{18,16},{20... | collective-permute-start | bytes 393224 | tf_op jit(solution)/shard_map/ppermute | solution.py:12
  110.5 10.9 %copy-start.22 = (f32[256,128]{0,1:T(8,128)S(1)}, f32[256,128]{0,1:T(8,128)}, u32[]{:S(2)}) copy-start(f32[256,128]{0,1:T(8,128)} %fusion.68) | copy-start | bytes 393220
  110.5 12.8 %copy-start.7 = (f32[256,256,8]{1,0,2:T(8,128)S(1)}, f32[256,256,8]{1,0,2:T(8,128)}, u32[]{:S(2)}) copy-start(f32[256,256,8]{1,0,2:T(8,128)} %copy-done.6) | copy-start | bytes 6291460
  114.2 7.2 %collective-permute-start.8 = (bf16[256,256]{0,1:T(8,128)(2,1)S(1)}, bf16[256,256]{0,1:T(8,128)(2,1)S(1)}, u32[]{:S(2)}, u32[]{:S(2)}) collective-permute-start(bf16[256,256]{0,1:T(8,128)(2,1)S(1)} %fusion.89), channel_id=1, source_target_pairs={{2,0},{4,2},{6,4},{8,6},{10,8},{12,10},{14,12},{16,14},{18,16},{20... | collective-permute-start | bytes 393224 | tf_op jit(solution)/shard_map/ppermute | solution.py:12
  116.6 12.0 %copy-start.21 = (f32[256,128]{0,1:T(8,128)S(1)}, f32[256,128]{0,1:T(8,128)}, u32[]{:S(2)}) copy-start(f32[256,128]{0,1:T(8,128)} %fusion.67) | copy-start | bytes 393220
  116.7 13.9 %copy-start.5 = (f32[256,256,8]{1,0,2:T(8,128)S(1)}, f32[256,256,8]{1,0,2:T(8,128)}, u32[]{:S(2)}) copy-start(f32[256,256,8]{1,0,2:T(8,128)} %copy-done.4) | copy-start | bytes 6291460
  121.4 7.2 %collective-permute-start.9 = (bf16[256,256]{0,1:T(8,128)(2,1)S(1)}, bf16[256,256]{0,1:T(8,128)(2,1)S(1)}, u32[]{:S(2)}, u32[]{:S(2)}) collective-permute-start(bf16[256,256]{0,1:T(8,128)(2,1)S(1)} %fusion.90), channel_id=1, source_target_pairs={{2,0},{4,2},{6,4},{8,6},{10,8},{12,10},{14,12},{16,14},{18,16},{20... | collective-permute-start | bytes 393224 | tf_op jit(solution)/shard_map/ppermute | solution.py:12
  123.9 12.0 %copy-start.20 = (f32[256,128]{0,1:T(8,128)S(1)}, f32[256,128]{0,1:T(8,128)}, u32[]{:S(2)}) copy-start(f32[256,128]{0,1:T(8,128)} %fusion.66) | copy-start | bytes 393220
  123.9 13.9 %copy-start.3 = (f32[256,256,8]{1,0,2:T(8,128)S(1)}, f32[256,256,8]{1,0,2:T(8,128)}, u32[]{:S(2)}) copy-start(f32[256,256,8]{1,0,2:T(8,128)} %copy-done.2) | copy-start | bytes 6291460
  128.6 7.2 %collective-permute-start.10 = (bf16[256,256]{0,1:T(8,128)(2,1)S(1)}, bf16[256,256]{0,1:T(8,128)(2,1)S(1)}, u32[]{:S(2)}, u32[]{:S(2)}) collective-permute-start(bf16[256,256]{0,1:T(8,128)(2,1)S(1)} %fusion.91), channel_id=1, source_target_pairs={{2,0},{4,2},{6,4},{8,6},{10,8},{12,10},{14,12},{16,14},{18,16},{20... | collective-permute-start | bytes 393224 | tf_op jit(solution)/shard_map/ppermute | solution.py:12
  131.1 13.9 %copy-start.1 = (f32[256,256,8]{1,0,2:T(8,128)S(1)}, f32[256,256,8]{1,0,2:T(8,128)}, u32[]{:S(2)}) copy-start(f32[256,256,8]{1,0,2:T(8,128)} %copy-done) | copy-start | bytes 6291460
  135.9 7.2 %collective-permute-start.11 = (bf16[256,256]{0,1:T(8,128)(2,1)S(1)}, bf16[256,256]{0,1:T(8,128)(2,1)S(1)}, u32[]{:S(2)}, u32[]{:S(2)}) collective-permute-start(bf16[256,256]{0,1:T(8,128)(2,1)S(1)} %fusion.92), channel_id=1, source_target_pairs={{2,0},{4,2},{6,4},{8,6},{10,8},{12,10},{14,12},{16,14},{18,16},{20... | collective-permute-start | bytes 393224 | tf_op jit(solution)/shard_map/ppermute | solution.py:12
  143.1 7.2 %collective-permute-start.12 = (bf16[256,256]{0,1:T(8,128)(2,1)S(1)}, bf16[256,256]{0,1:T(8,128)(2,1)S(1)}, u32[]{:S(2)}, u32[]{:S(2)}) collective-permute-start(bf16[256,256]{0,1:T(8,128)(2,1)S(1)} %fusion.93), channel_id=1, source_target_pairs={{2,0},{4,2},{6,4},{8,6},{10,8},{12,10},{14,12},{16,14},{18,16},{20... | collective-permute-start | bytes 393224 | tf_op jit(solution)/shard_map/ppermute | solution.py:12
  150.3 7.2 %collective-permute-start.13 = (bf16[256,256]{0,1:T(8,128)(2,1)S(1)}, bf16[256,256]{0,1:T(8,128)(2,1)S(1)}, u32[]{:S(2)}, u32[]{:S(2)}) collective-permute-start(bf16[256,256]{0,1:T(8,128)(2,1)S(1)} %fusion.94), channel_id=1, source_target_pairs={{2,0},{4,2},{6,4},{8,6},{10,8},{12,10},{14,12},{16,14},{18,16},{20... | collective-permute-start | bytes 393224 | tf_op jit(solution)/shard_map/ppermute | solution.py:12
where the time goes:
time: 171 us; the launch traced here: 170 us
  starting transfers between devices  45.7 us (27%)
  waiting for transfers between devices  40.7 us (24%)
  matrix products  36.4 us (21%)
  other arithmetic  15.5 us (9%)
  between operations  14.1 us (8%)
  blocking collectives  11 us (6%)
  local copies, waits for them, and re-layouts  6.58 us (4%)
    ppermute x14, starting transfers between devices, from_behind(): return lax.ppermute(array, axis, pairs)  45.7 us
    ppermute x14, waiting for transfers between devices, from_behind(): return lax.ppermute(array, axis, pairs)  40.7 us
    dot_general x8, matrix products, local(): jnp.einsum('ihd,jd->hij', grad_heads, first_tile[:, width:], preferred_el...  14.6 us
    convert_element_type x1, other arithmetic, grad_step(): grad_low = grad_scores.astype(jnp.bfloat16)  12.2 us
    psum x1, blocking collectives, local(): result = lax.psum(carried, 'head').astype(jnp.bfloat16)  11 us
    dot_general x8, matrix products, grad_step(): jnp.einsum('hij,ihd->jd', grad_low, query_heads, preferred_element_type=j...  8.35 us
    dot_general x8, matrix products, grad_step(): jnp.einsum('hij,ihd->jd', probs_low, grad_heads, preferred_element_type=j...  6.2 us
    dot_general x8, matrix products, local(): jnp.einsum('ihd,jd->hij', query_heads, first_tile[:, :width], preferred_e...  4.37 us
  transfers between devices with their start and end apart: 14, of which 13 were waited for; matrix products, arithmetic and copies ran while one was open for 8% of the time, Pallas kernels for 0%

commit v1 on v0

v1 whole, which is shorter than its diff:
```python
import functools
import math

import jax
import jax.numpy as jnp
from jax import lax
from jax.experimental import pallas as pl
from jax.experimental.pallas import tpu as pltpu
from jax.sharding import PartitionSpec as P

NEG = -1e30
BIG = 1e30
MESH = pl.DeviceIdType.MESH
F32 = jnp.float32
BF16 = jnp.bfloat16


def transposed(x):
    return x.astype(F32).T.astype(BF16)


def kernel(
    n, parts, reach, heads, rows, width,
    q, k, v, g, doc, pair, knock,
    dq, dk, dv,
    kv, qt, gt, e_s, dp_s, tops, top, total, weighted, dqt,
    pf, part, rx, red, rc, fin,
    gather_send, gather_recv, pass_send, pass_recv,
    part_send, part_recv, back_send, back_recv, fin_send, fin_recv,
):
    here = lax.axis_index("ctx")
    mine = lax.axis_index("head")
    scale = width ** (-0.5)
    coef = scale * math.log2(math.e)
    share = 2 * rows // parts
    slots = jnp.minimum(here + 1, reach)
    after = jnp.minimum(n - 1 - here, reach - 1)
    my_rows = pl.ds(pl.multiple_of(mine * share, share), share)

    def peer(t):
        return lax.rem(mine + t, parts)

    def rows_of(index):
        return pl.ds(pl.multiple_of(index * share, share), share)

    def gather_copy(d):
        return pltpu.make_async_remote_copy(
            src_ref=kv.at[0, my_rows], dst_ref=kv.at[d, my_rows],
            send_sem=gather_send.at[d], recv_sem=gather_recv.at[d],
            device_id={"ctx": lax.rem(here + d, n)}, device_id_type=MESH)

    def pass_copy(d, t):
        return pltpu.make_async_remote_copy(
            src_ref=kv.at[d, my_rows], dst_ref=kv.at[d, my_rows],
            send_sem=pass_send.at[d, t - 1], recv_sem=pass_recv.at[d, t - 1],
            device_id={"head": peer(t)}, device_id_type=MESH)

    def pass_arrival(d, t):
        theirs = rows_of(lax.rem(mine + parts - t, parts))
        return pltpu.make_async_remote_copy(
            src_ref=kv.at[d, theirs], dst_ref=kv.at[d, theirs],
            send_sem=pass_send.at[d, t - 1], recv_sem=pass_recv.at[d, t - 1],
            device_id={"head": peer(t)}, device_id_type=MESH)

    def part_copy(o, t):
        return pltpu.make_async_remote_copy(
            src_ref=part.at[o, rows_of(peer(t))], dst_ref=rx.at[o, t - 1],
            send_sem=part_send.at[o, t - 1], recv_sem=part_recv.at[o, t - 1],
            device_id={"head": peer(t)}, device_id_type=MESH)

    def back_copy(o):
        return pltpu.make_async_remote_copy(
            src_ref=red.at[o], dst_ref=rc.at[o],
            send_sem=back_send.at[o], recv_sem=back_recv.at[o],
            device_id={"ctx": lax.rem(here + n - o, n)}, device_id_type=MESH)

    def fin_copy(t):
        return pltpu.make_async_remote_copy(
            src_ref=fin.at[my_rows], dst_ref=fin.at[my_rows],
            send_sem=fin_send.at[t - 1], recv_sem=fin_recv.at[t - 1],
            device_id={"head": peer(t)}, device_id_type=MESH)

    def fin_arrival(t):
        theirs = rows_of(lax.rem(mine + parts - t, parts))
        return pltpu.make_async_remote_copy(
            src_ref=fin.at[theirs], dst_ref=fin.at[theirs],
            send_sem=fin_send.at[t - 1], recv_sem=fin_recv.at[t - 1],
            device_id={"head": peer(t)}, device_id_type=MESH)

    barrier = pltpu.get_barrier_semaphore()

    def greet(d, _):
        @pl.when(d <= after)
        def _():
            pl.semaphore_signal(barrier, inc=1, device_id={"ctx": lax.rem(here + d, n)}, device_id_type=MESH)

        @pl.when(d < slots)
        def _():
            pl.semaphore_signal(barrier, inc=1, device_id={"ctx": lax.rem(here + n - d, n)}, device_id_type=MESH)

        return 0

    lax.fori_loop(1, reach, greet, 0)
    for t in range(1, parts):
        pl.semaphore_signal(barrier, inc=1, device_id={"head": peer(t)}, device_id_type=MESH)
    kv[0, 0:rows, :] = k[...]
    kv[0, rows:2 * rows, :] = v[...]
    pl.semaphore_wait(barrier, after + slots - 1 + parts - 1)

    def send_block(d, _):
        gather_copy(d).start()
        return 0

    lax.fori_loop(1, after + 1, send_block, 0)

    for h in range(heads):
        qt[:, h * rows:(h + 1) * rows] = transposed(q[:, h * width:(h + 1) * width])
        gt[:, h * rows:(h + 1) * rows] = transposed(g[:, h * width:(h + 1) * width])
    dqt[...] = jnp.zeros_like(dqt)

    def forward(d):
        gather_copy(d).wait_recv()
        for t in range(1, parts):
            pass_copy(d, t).start()

    def score_slot(o, own):
        keys = kv[o, 0:rows, :]
        values = kv[o, rows:2 * rows, :]
        if own:
            lower = (lax.broadcasted_iota(jnp.int32, (rows, rows), 0)
                     <= lax.broadcasted_iota(jnp.int32, (rows, rows), 1))
        else:
            source = here - o
            listed = jnp.int32(0)
            for j in range(reach - 1):
                listed = listed + (pair[0, j] == o).astype(jnp.int32)
            allowed = jnp.minimum(listed, 1) * (doc[source] == doc[here]).astype(jnp.int32)
        for h in range(heads):
            cols = slice(h * rows, (h + 1) * rows)
            raw = jnp.dot(keys, qt[:, cols], preferred_element_type=F32)
            grad_probs = jnp.dot(values, gt[:, cols], preferred_element_type=F32)
            if own:
                raw = jnp.where(lower, raw, NEG)
                now = jnp.max(raw, axis=0, keepdims=True) * coef
                shifted = jnp.exp2(raw * coef - now)
                total[h:h + 1, :] = jnp.sum(shifted, axis=0, keepdims=True)
                weighted[h:h + 1, :] = jnp.sum(shifted * grad_probs, axis=0, keepdims=True)
            else:
                live = jnp.full((1, rows), allowed * knock[h, source], jnp.int32) == 1
                before = top[h:h + 1, :]
                now = jnp.where(
                    live, jnp.maximum(before, jnp.max(raw, axis=0, keepdims=True) * coef), before)
                factor = jnp.exp2(before - now)
                shifted = jnp.exp2(raw * coef - jnp.where(live, now, BIG))
                total[h:h + 1, :] = total[h:h + 1, :] * factor + jnp.sum(shifted, axis=0, keepdims=True)
                weighted[h:h + 1, :] = (
                    weighted[h:h + 1, :] * factor + jnp.sum(shifted * grad_probs, axis=0, keepdims=True))
            top[h:h + 1, :] = now
            tops[o, h:h + 1, :] = now
            e_s[o, :, cols] = shifted
            dp_s[o, :, cols] = grad_probs

    @pl.when(slots > 1)
    def _():
        forward(1)

    score_slot(0, True)

    def score_step(o, _):
        @pl.when(o + 1 < slots)
        def _():
            forward(o + 1)

        for t in range(1, parts):
            pass_arrival(o, t).wait_recv()
        score_slot(o, False)
        return 0

    lax.fori_loop(1, slots, score_step, 0)
    total[...] = 1.0 / total[...]
    weighted[...] = weighted[...] * total[...]

    def grad_slot(o):
        keys_t = transposed(kv[o, 0:rows, :])
        key_part = jnp.zeros((rows, width), F32)
        value_part = jnp.zeros((rows, width), F32)
        for h in range(heads):
            cols = slice(h * rows, (h + 1) * rows)
            lanes = slice(h * width, (h + 1) * width)
            factor = jnp.exp2(tops[o, h:h + 1, :] - top[h:h + 1, :]) * total[h:h + 1, :]
            probs = e_s[o, :, cols] * factor
            grad_scores = probs * (dp_s[o, :, cols] - weighted[h:h + 1, :])
            probs_low = probs.astype(BF16)
            grad_low = grad_scores.astype(BF16)
            key_part += jnp.dot(grad_low, q[:, lanes], preferred_element_type=F32)
            value_part += jnp.dot(probs_low, g[:, lanes], preferred_element_type=F32)
            dqt[:, cols] += jnp.dot(keys_t, grad_low, preferred_element_type=F32)
        key_part = key_part * scale
        pf[o, 0:rows, :] = key_part
        pf[o, rows:2 * rows, :] = value_part
        part[o, 0:rows, :] = key_part.astype(BF16)
        part[o, rows:2 * rows, :] = value_part.astype(BF16)

    def head_sum(o):
        out = pf[o, my_rows, :]
        for t in range(1, parts):
            part_copy(o, t).wait_recv()
            out = out + rx[o, t - 1].astype(F32)
        return out

    def send_back(o):
        red[o] = head_sum(o).astype(BF16)
        back_copy(o).start()

    def grad_step(i, _):
        o = slots - 1 - i
        grad_slot(o)
        for t in range(1, parts):
            part_copy(o, t).start()

        @pl.when(i > 0)
        def _():
            send_back(o + 1)

        return 0

    lax.fori_loop(0, slots, grad_step, 0)

    for h in range(heads):
        block = dqt[:, h * rows:(h + 1) * rows] * scale
        dq[:, h * width:(h + 1) * width] = block.T.astype(BF16)

    def take(d, out):
        back_copy(d).wait_recv()
        return out + rc[d].astype(F32)

    result = lax.fori_loop(1, after + 1, take, head_sum(0))
    fin[my_rows, :] = result.astype(BF16)
    for t in range(1, parts):
        fin_copy(t).start()
    for t in range(1, parts):
        fin_arrival(t).wait_recv()
    dk[...] = fin[0:rows, :]
    dv[...] = fin[rows:2 * rows, :]

    def sent_blocks(d, _):
        gather_copy(d).wait_send()
        return 0

    lax.fori_loop(1, after + 1, sent_blocks, 0)

    def sent_slots(o, _):
        for t in range(1, parts):
            part_copy(o, t).wait_send()

        @pl.when(o > 0)
        def _():
            back_copy(o).wait_send()
            for t in range(1, parts):
                pass_copy(o, t).wait_send()

        return 0

    lax.fori_loop(0, slots, sent_slots, 0)
    for t in range(1, parts):
        fin_copy(t).wait_send()


def local(n, parts, queries, keys, values, grad_out, doc_of_block, pair_list, knock):
    rows, width = keys.shape
    heads = queries.shape[1] // width
    reach = min(pair_list.shape[1] + 1, n)
    share = 2 * rows // parts
    others = parts - 1
    vmem = pl.BlockSpec(memory_space=pltpu.VMEM)
    smem = pl.BlockSpec(memory_space=pltpu.SMEM)
    dma = pltpu.SemaphoreType.DMA
    tiles = reach * heads * rows * rows
    return pl.pallas_call(
        functools.partial(kernel, n, parts, reach, heads, rows, width),
        out_shape=(
            jax.ShapeDtypeStruct(queries.shape, BF16),
            jax.ShapeDtypeStruct(keys.shape, BF16),
            jax.ShapeDtypeStruct(values.shape, BF16),
        ),
        in_specs=[vmem] * 4 + [smem] * 3,
        out_specs=(vmem,) * 3,
        scratch_shapes=[
            pltpu.VMEM((reach, 2 * rows, width), BF16),
            pltpu.VMEM((width, heads * rows), BF16),
            pltpu.VMEM((width, heads * rows), BF16),
            pltpu.VMEM((reach, rows, heads * rows), F32),
            pltpu.VMEM((reach, rows, heads * rows), F32),
            pltpu.VMEM((reach, heads, rows), F32),
            pltpu.VMEM((heads, rows), F32),
            pltpu.VMEM((heads, rows), F32),
            pltpu.VMEM((heads, rows), F32),
            pltpu.VMEM((width, heads * rows), F32),
            pltpu.VMEM((reach, 2 * rows, width), F32),
            pltpu.VMEM((reach, 2 * rows, width), BF16),
            pltpu.VMEM((reach, others, share, width), BF16),
            pltpu.VMEM((reach, share, width), BF16),
            pltpu.VMEM((reach, share, width), BF16),
            pltpu.VMEM((2 * rows, width), BF16),
            dma((reach,)), dma((reach,)),
            dma((reach, others)), dma((reach, others)),
            dma((reach, others)), dma((reach, others)),
            dma((reach,)), dma((reach,)),
            dma((others,)), dma((others,)),
        ],
        compiler_params=pltpu.CompilerParams(
            collective_id=0, has_side_effects=True, vmem_limit_bytes=56 * 1024 * 1024),
        cost_estimate=pl.CostEstimate(
            flops=10 * tiles * width, bytes_accessed=4 * 2 * rows * heads * width, transcendentals=tiles),
    )(queries, keys, values, grad_out, doc_of_block, pair_list, knock)


def solution(mesh):
    in_specs = (
        P("ctx", "head"),
        P("ctx", None),
        P("ctx", None),
        P("ctx", "head"),
        P(),
        P("ctx", None),
        P("head", None),
    )
    out_specs = (P("ctx", "head"), P("ctx", None), P("ctx", None))
    body = functools.partial(local, mesh.shape["ctx"], mesh.shape["head"])
    return jax.shard_map(body, mesh=mesh, in_specs=in_specs, out_specs=out_specs, check_vma=False)
```

time: 171 us -> 55.8 us (0.33)
  the two profiles are of different devices: /device:TPU:21 before, /device:TPU:13 now
where the time goes in v1:
time: 55.8 us; the launch traced here: 55.6 us
  Pallas kernels  51.6 us (92%)
  local copies, waits for them, and re-layouts  3.4 us (6%)
  between operations  0.65 us (1%)
    pallas_call x1, Pallas kernels, local(): pl.pallas_call(functools.partial(kernel, n, parts, reach, heads, rows, wi...  51.6 us
    unnamed x7, local copies, waits for them, and re-layouts  3.4 us

profile of v1, /device:TPU:13, one launch (start us, length us, event | category | flops | bytes accessed | tf_op | source)
XLA Modules:
  0.0 55.6 jit_solution(7910064324698888566)
XLA Ops:
  0.6 51.6 %shard_map.94 = (bf16[256,1024]{1,0:T(8,128)(2,1)}, bf16[256,128]{1,0:T(8,128)(2,1)}, bf16[256,128]{1,0:T(8,128)(2,1)}) custom-call(bf16[256,1024]{1,0:T(8,128)(2,1)} %q.1, bf16[256,128]{1,0:T(8,128)(2,1)} %k.1, bf16[256,128]{1,0:T(8,128)(2,1)} %v.1, bf16[256,1024]{1,0:T(8,128)(2,1)} %g.1, s32[16]{0:T(128)} %doc.1, s32[1,7]{1,0:T(1,128)} %pair.1, s32[8,16]{1,0:T(8,128)} %knock.1), custom_call_target="tpu_custom_call" | custom-call | flops 5368709120 | bytes 2097152 | tf_op jit(solution)/shard_map/pallas_call | solution.py:279
  52.2 0.0 copy-start.1
  52.2 1.9 %copy.13 = bf16[256,1024]{1,0:T(8,128)(2,1)} copy(bf16[256,1024]{1,0:T(8,128)(2,1)} %get-tuple-element.6) | data formatting | bytes 1048576
  54.1 0.0 copy-done.1
  54.1 0.0 copy-start
  54.1 0.6 %copy.14 = bf16[256,128]{1,0:T(8,128)(2,1)} copy(bf16[256,128]{1,0:T(8,128)(2,1)S(1)} %copy-done.1) | data formatting | bytes 131072
  54.7 0.2 copy-done
  55.0 0.6 %copy.15 = bf16[256,128]{1,0:T(8,128)(2,1)} copy(bf16[256,128]{1,0:T(8,128)(2,1)S(1)} %copy-done) | data formatting | bytes 131072
Async XLA Ops:
  52.2 1.9 %copy-start.1 = (bf16[256,128]{1,0:T(8,128)(2,1)S(1)}, bf16[256,128]{1,0:T(8,128)(2,1)}, u32[]{:S(2)}) copy-start(bf16[256,128]{1,0:T(8,128)(2,1)} %get-tuple-element.7) | copy-start | bytes 196612
  54.1 0.9 %copy-start = (bf16[256,128]{1,0:T(8,128)(2,1)S(1)}, bf16[256,128]{1,0:T(8,128)(2,1)}, u32[]{:S(2)}) copy-start(bf16[256,128]{1,0:T(8,128)(2,1)} %get-tuple-element.8) | copy-start | bytes 196612

commit v2 on v1

--- a/solution.py
+++ b/solution.py
@@ -24,8 +24,9 @@
     q, k, v, g, doc, pair, knock,
     dq, dk, dv,
     kv, qt, gt, e_s, dp_s, tops, top, total, weighted, dqt,
-    pf, part, rx, red, rc, fin,
-    gather_send, gather_recv, pass_send, pass_recv,
+    pf, part, sx, rx, red, rc, fin,
+    gather_send, gather_recv, pass_send, pass_recv, twin_send, twin_recv,
+    mate_send, mate_recv,
     part_send, part_recv, back_send, back_recv, fin_send, fin_recv,
 ):
     here = lax.axis_index("ctx")
@@ -33,8 +34,10 @@
     scale = width ** (-0.5)
     coef = scale * math.log2(math.e)
     share = 2 * rows // parts
-    slots = jnp.minimum(here + 1, reach)
-    after = jnp.minimum(n - 1 - here, reach - 1)
+    side = lax.rem(here, 2)
+    twin = here + 1 - 2 * side
+    last = reach - 1
+    evens = tuple(range(2, reach, 2))
     my_rows = pl.ds(pl.multiple_of(mine * share, share), share)
 
     def peer(t):
@@ -87,41 +90,80 @@
             send_sem=fin_send.at[t - 1], recv_sem=fin_recv.at[t - 1],
             device_id={"head": peer(t)}, device_id_type=MESH)
 
+    def twin_copy(r):
+        return pltpu.make_async_remote_copy(
+            src_ref=kv.at[r], dst_ref=kv.at[r + 1 - 2 * side],
+            send_sem=twin_send.at[r], recv_sem=twin_recv.at[r + 1 - 2 * side],
+            device_id={"ctx": twin}, device_id_type=MESH)
+
+    def twin_arrival(o):
+        return pltpu.make_async_remote_copy(
+            src_ref=kv.at[o], dst_ref=kv.at[o],
+            send_sem=twin_send.at[o], recv_sem=twin_recv.at[o],
+            device_id={"ctx": twin}, device_id_type=MESH)
+
+    def mate_copy(o):
+        return pltpu.make_async_remote_copy(
+            src_ref=part.at[o], dst_ref=sx.at[o + 1 - 2 * side],
+            send_sem=mate_send.at[o], recv_sem=mate_recv.at[o + 1 - 2 * side],
+            device_id={"ctx": twin}, device_id_type=MESH)
+
+    def mate_arrival(r):
+        return pltpu.make_async_remote_copy(
+            src_ref=part.at[r], dst_ref=sx.at[r],
+            send_sem=mate_send.at[r], recv_sem=mate_recv.at[r],
+            device_id={"ctx": twin}, device_id_type=MESH)
+
+    ahead = [(r, here + r < n) for r in evens] + [(last, (here + last < n) & (side == 1))]
+    behind = [(r, here >= r) for r in evens] + [(last, (here >= last) & (side == 0))]
+
     barrier = pltpu.get_barrier_semaphore()
-
-    def greet(d, _):
-        @pl.when(d <= after)
-        def _():
-            pl.semaphore_signal(barrier, inc=1, device_id={"ctx": lax.rem(here + d, n)}, device_id_type=MESH)
-
-        @pl.when(d < slots)
-        def _():
-            pl.semaphore_signal(barrier, inc=1, device_id={"ctx": lax.rem(here + n - d, n)}, device_id_type=MESH)
-
-        return 0
-
-    lax.fori_loop(1, reach, greet, 0)
+    greeted = jnp.int32(parts)
+    for r, there in ahead:
+        greeted = greeted + there.astype(jnp.int32)
+
+        @pl.when(there)
+        def _():
+            pl.semaphore_signal(barrier, inc=1, device_id={"ctx": lax.rem(here + r, n)}, device_id_type=MESH)
+
+    for r, there in behind:
+        greeted = greeted + there.astype(jnp.int32)
+
+        @pl.when(there)
+        def _():
+            pl.semaphore_signal(barrier, inc=1, device_id={"ctx": lax.rem(here + n - r, n)}, device_id_type=MESH)
+
+    pl.semaphore_signal(barrier, inc=1, device_id={"ctx": twin}, device_id_type=MESH)
     for t in range(1, parts):
         pl.semaphore_signal(barrier, inc=1, device_id={"head": peer(t)}, device_id_type=MESH)
     kv[0, 0:rows, :] = k[...]
     kv[0, rows:2 * rows, :] = v[...]
-    pl.semaphore_wait(barrier, after + slots - 1 + parts - 1)
-
-    def send_block(d, _):
-        gather_copy(d).start()
-        return 0
-
-    lax.fori_loop(1, after + 1, send_block, 0)
+    pl.semaphore_wait(barrier, greeted)
+
+    for r, there in ahead:
+        @pl.when(there)
+        def _():
+            gather_copy(r).start()
+
+    @pl.when(side == 0)
+    def _():
+        twin_copy(0).start()
 
     for h in range(heads):
         qt[:, h * rows:(h + 1) * rows] = transposed(q[:, h * width:(h + 1) * width])
         gt[:, h * rows:(h + 1) * rows] = transposed(g[:, h * width:(h + 1) * width])
     dqt[...] = jnp.zeros_like(dqt)
 
-    def forward(d):
-        gather_copy(d).wait_recv()
+    def forward(r, there):
+        @pl.when(there)
+        def _():
+            gather_copy(r).wait_recv()
+            for t in range(1, parts):
+                pass_copy(r, t).start()
+
+    def gathered(r):
         for t in range(1, parts):
-            pass_copy(d, t).start()
+            pass_arrival(r, t).wait_recv()
 
     def score_slot(o, own):
         keys = kv[o, 0:rows, :]
@@ -160,23 +202,45 @@
             e_s[o, :, cols] = shifted
             dp_s[o, :, cols] = grad_probs
 
-    @pl.when(slots > 1)
-    def _():
-        forward(1)
-
+    def slot_at(t):
+        inner = jnp.where(lax.rem(t, 2) == 1, t + 1, jnp.maximum(t - 1, 0))
+        return jnp.where((side == 1) | (t == last), t, inner)
+
+    forward(*behind[0])
     score_slot(0, True)
 
-    def score_step(o, _):
-        @pl.when(o + 1 < slots)
-        def _():
-            forward(o + 1)
-
-        for t in range(1, parts):
-            pass_arrival(o, t).wait_recv()
-        score_slot(o, False)
+    def score_step(t, _):
+        o = slot_at(t)
+
+        @pl.when(lax.rem(t, 2) == 1)
+        def _():
+            r = t + 1
+
+            @pl.when((r <= here) & (r < reach))
+            def _():
+                gathered(r)
+                twin_copy(r).start()
+
+            for j in range(1, len(behind)):
+                @pl.when(t == 2 * j - 1)
+                def _():
+                    forward(*behind[j])
+
+        @pl.when(o <= here)
+        def _():
+            @pl.when((lax.rem(o, 2) == 1) & ((side == 1) | (o < last)))
+            def _():
+                twin_arrival(o).wait_recv()
+
+            @pl.when((side == 0) & (o == last))
+            def _():
+                gathered(o)
+
+            score_slot(o, False)
+
         return 0
 
-    lax.fori_loop(1, slots, score_step, 0)
+    lax.fori_loop(1, reach, score_step, 0)
     total[...] = 1.0 / total[...]
     weighted[...] = weighted[...] * total[...]
 
@@ -208,34 +272,76 @@
             out = out + rx[o, t - 1].astype(F32)
         return out
 
+    def send_parts(o):
+        for t in range(1, parts):
+            part_copy(o, t).start()
+
+    def join_twin(r):
+        @pl.when((r > 0) | (side == 0))
+        def _():
+            mate_arrival(r).wait_recv()
+            both = pf[r] + sx[r].astype(F32)
+            pf[r] = both
+            part[r] = both.astype(BF16)
+
+        send_parts(r)
+
     def send_back(o):
         red[o] = head_sum(o).astype(BF16)
         back_copy(o).start()
 
     def grad_step(i, _):
-        o = slots - 1 - i
-        grad_slot(o)
-        for t in range(1, parts):
-            part_copy(o, t).start()
-
-        @pl.when(i > 0)
-        def _():
-            send_back(o + 1)
+        o = slot_at(last - i)
+
+        @pl.when(o <= here)
+        def _():
+            grad_slot(o)
+
+            @pl.when((lax.rem(o, 2) == 1) & ((side == 1) | (o < last)))
+            def _():
+                mate_copy(o).start()
+
+            @pl.when((side == 0) & (o == last))
+            def _():
+                send_parts(o)
+
+        u = i - 1 + side
+
+        @pl.when(lax.rem(u, 2) == 0)
+        def _():
+            @pl.when((u >= 2) & (reach - u <= here))
+            def _():
+                join_twin(reach - u)
+
+            @pl.when((u >= 4) & (reach + 2 - u <= here))
+            def _():
+                send_back(reach + 2 - u)
+
+        @pl.when((side == 0) & (i == 2) & (here >= last))
+        def _():
+            send_back(jnp.int32(last))
 
         return 0
 
-    lax.fori_loop(0, slots, grad_step, 0)
+    lax.fori_loop(0, reach, grad_step, 0)
+    join_twin(0)
+
+    @pl.when(here >= 2)
+    def _():
+        send_back(2)
 
     for h in range(heads):
         block = dqt[:, h * rows:(h + 1) * rows] * scale
         dq[:, h * width:(h + 1) * width] = block.T.astype(BF16)
 
-    def take(d, out):
-        back_copy(d).wait_recv()
-        return out + rc[d].astype(F32)
-
-    result = lax.fori_loop(1, after + 1, take, head_sum(0))
-    fin[my_rows, :] = result.astype(BF16)
+    pf[0, my_rows, :] = head_sum(0)
+    for r, there in reversed(ahead):
+        @pl.when(there)
+        def _():
+            back_copy(r).wait_recv()
+            pf[0, my_rows, :] += rc[r].astype(F32)
+
+    fin[my_rows, :] = pf[0, my_rows, :].astype(BF16)
     for t in range(1, parts):
         fin_copy(t).start()
     for t in range(1, parts):
@@ -243,27 +349,41 @@
     dk[...] = fin[0:rows, :]
     dv[...] = fin[rows:2 * rows, :]
 
-    def sent_blocks(d, _):
-        gather_copy(d).wait_send()
-        return 0
-
-    lax.fori_loop(1, after + 1, sent_blocks, 0)
-
-    def sent_slots(o, _):
-        for t in range(1, parts):
-            part_copy(o, t).wait_send()
-
-        @pl.when(o > 0)
-        def _():
-            back_copy(o).wait_send()
+    for r, there in ahead:
+        @pl.when(there)
+        def _():
+            gather_copy(r).wait_send()
+
+    for r, there in behind:
+        @pl.when(there)
+        def _():
+            back_copy(r).wait_send()
             for t in range(1, parts):
-                pass_copy(o, t).wait_send()
-
-        return 0
-
-    lax.fori_loop(0, slots, sent_slots, 0)
+                pass_copy(r, t).wait_send()
+                part_copy(r, t).wait_send()
+
     for t in range(1, parts):
+        part_copy(0, t).wait_send()
         fin_copy(t).wait_send()
+    for r in (0,) + evens:
+        @pl.when((here >= r) & ((r > 0) | (side == 0)))
+        def _():
+            twin_copy(r).wait_send()
+
+    for o in range(1, reach, 2):
+        @pl.when((o <= here) & ((side == 1) | (o < last)))
+        def _():
+            mate_copy(o).wait_send()
+
+
+def finish(*refs):
+    count = (len(refs) - 1) // 2
+    sems = refs[-1]
+    copies = [pltpu.make_async_copy(refs[i], refs[count + i], sems.at[i]) for i in range(count)]
+    for copy in copies:
+        copy.start()
+    for copy in copies:
+        copy.wait()
 
 
 def local(n, parts, queries, keys, values, grad_out, doc_of_block, pair_list, knock):
@@ -276,7 +396,7 @@
     smem = pl.BlockSpec(memory_space=pltpu.SMEM)
     dma = pltpu.SemaphoreType.DMA
     tiles = reach * heads * rows * rows
-    return pl.pallas_call(
+    results = pl.pallas_call(
         functools.partial(kernel, n, parts, reach, heads, rows, width),
         out_shape=(
             jax.ShapeDtypeStruct(queries.shape, BF16),
@@ -298,12 +418,15 @@
             pltpu.VMEM((width, heads * rows), F32),
             pltpu.VMEM((reach, 2 * rows, width), F32),
             pltpu.VMEM((reach, 2 * rows, width), BF16),
+            pltpu.VMEM((reach, 2 * rows, width), BF16),
             pltpu.VMEM((reach, others, share, width), BF16),
             pltpu.VMEM((reach, share, width), BF16),
             pltpu.VMEM((reach, share, width), BF16),
             pltpu.VMEM((2 * rows, width), BF16),
             dma((reach,)), dma((reach,)),
             dma((reach, others)), dma((reach, others)),
+            dma((reach,)), dma((reach,)),
+            dma((reach,)), dma((reach,)),
             dma((reach, others)), dma((reach, others)),
             dma((reach,)), dma((reach,)),
             dma((others,)), dma((others,)),
@@ -313,6 +436,15 @@
         cost_estimate=pl.CostEstimate(
             flops=10 * tiles * width, bytes_accessed=4 * 2 * rows * heads * width, transcendentals=tiles),
     )(queries, keys, values, grad_out, doc_of_block, pair_list, knock)
+    anywhere = pl.BlockSpec(memory_space=pl.ANY)
+    return pl.pallas_call(
+        finish,
+        out_shape=tuple(jax.ShapeDtypeStruct(x.shape, x.dtype) for x in results),
+        in_specs=[anywhere] * 3,
+        out_specs=(anywhere,) * 3,
+        scratch_shapes=[dma((3,))],
+        compiler_params=pltpu.CompilerParams(vmem_limit_bytes=56 * 1024 * 1024),
+    )(*results)
 
 
 def solution(mesh):

time: 55.8 us -> 67.2 us (1.20)
  the two profiles are of different devices: /device:TPU:13 before, /device:TPU:12 now
where the time goes in v2:
time: 67.2 us; the launch traced here: 66.5 us
  Pallas kernels  65.9 us (98%)
    pallas_call x1, Pallas kernels, local(): pl.pallas_call(functools.partial(kernel, n, parts, reach, heads, rows, wi...  44.9 us
    pallas_call x1, Pallas kernels, local(): pl.pallas_call(finish, out_shape=tuple((jax.ShapeDtypeStruct(x.shape, x.d...  21 us

profile of v2, /device:TPU:12, one launch (start us, length us, event | category | flops | bytes accessed | tf_op | source)
XLA Modules:
  0.0 66.5 jit_solution(5224486758151828911)
XLA Ops:
  0.6 44.9 %shard_map.94 = (bf16[256,1024]{1,0:T(8,128)(2,1)}, bf16[256,128]{1,0:T(8,128)(2,1)}, bf16[256,128]{1,0:T(8,128)(2,1)}) custom-call(bf16[256,1024]{1,0:T(8,128)(2,1)} %q.1, bf16[256,128]{1,0:T(8,128)(2,1)} %k.1, bf16[256,128]{1,0:T(8,128)(2,1)} %v.1, bf16[256,1024]{1,0:T(8,128)(2,1)} %g.1, s32[16]{0:T(128)} %doc.1, s32[1,7]{1,0:T(1,128)} %pair.1, s32[8,16]{1,0:T(8,128)} %knock.1), custom_call_target="tpu_custom_call" | custom-call | flops 5368709120 | bytes 2097152 | tf_op jit(solution)/shard_map/pallas_call | solution.py:399
  45.5 21.0 %shard_map.95 = (bf16[256,1024]{1,0:T(8,128)(2,1)}, bf16[256,128]{1,0:T(8,128)(2,1)}, bf16[256,128]{1,0:T(8,128)(2,1)}) custom-call(bf16[256,1024]{1,0:T(8,128)(2,1)} %get-tuple-element.6.refs_0_, bf16[256,128]{1,0:T(8,128)(2,1)} %get-tuple-element.7.refs_1_, bf16[256,128]{1,0:T(8,128)(2,1)} %get-tuple-element.8.refs_2_), custom_call_target="tpu_custom_call" | custom-call | tf_op jit(solution)/shard_map/pallas_call | solution.py:440

commit v3 on v2

--- a/solution.py
+++ b/solution.py
@@ -23,7 +23,7 @@
     n, parts, reach, heads, rows, width,
     q, k, v, g, doc, pair, knock,
     dq, dk, dv,
-    kv, qt, gt, e_s, dp_s, tops, top, total, weighted, dqt,
+    kv, qt, gt, qs, gs, p_low, g_low, e_s, dp_s, tops, top, total, weighted, dqt,
     pf, part, sx, rx, red, rc, fin,
     gather_send, gather_recv, pass_send, pass_recv, twin_send, twin_recv,
     mate_send, mate_recv,
@@ -152,6 +152,8 @@
     for h in range(heads):
         qt[:, h * rows:(h + 1) * rows] = transposed(q[:, h * width:(h + 1) * width])
         gt[:, h * rows:(h + 1) * rows] = transposed(g[:, h * width:(h + 1) * width])
+        qs[h * rows:(h + 1) * rows, :] = q[:, h * width:(h + 1) * width]
+        gs[h * rows:(h + 1) * rows, :] = g[:, h * width:(h + 1) * width]
     dqt[...] = jnp.zeros_like(dqt)
 
     def forward(r, there):
@@ -246,20 +248,16 @@
 
     def grad_slot(o):
         keys_t = transposed(kv[o, 0:rows, :])
-        key_part = jnp.zeros((rows, width), F32)
-        value_part = jnp.zeros((rows, width), F32)
         for h in range(heads):
             cols = slice(h * rows, (h + 1) * rows)
-            lanes = slice(h * width, (h + 1) * width)
             factor = jnp.exp2(tops[o, h:h + 1, :] - top[h:h + 1, :]) * total[h:h + 1, :]
             probs = e_s[o, :, cols] * factor
             grad_scores = probs * (dp_s[o, :, cols] - weighted[h:h + 1, :])
-            probs_low = probs.astype(BF16)
-            grad_low = grad_scores.astype(BF16)
-            key_part += jnp.dot(grad_low, q[:, lanes], preferred_element_type=F32)
-            value_part += jnp.dot(probs_low, g[:, lanes], preferred_element_type=F32)
-            dqt[:, cols] += jnp.dot(keys_t, grad_low, preferred_element_type=F32)
-        key_part = key_part * scale
+            p_low[:, cols] = probs.astype(BF16)
+            g_low[:, cols] = grad_scores.astype(BF16)
+        key_part = jnp.dot(g_low[...], qs[...], preferred_element_type=F32) * scale
+        value_part = jnp.dot(p_low[...], gs[...], preferred_element_type=F32)
+        dqt[...] += jnp.dot(keys_t, g_low[...], preferred_element_type=F32)
         pf[o, 0:rows, :] = key_part
         pf[o, rows:2 * rows, :] = value_part
         part[o, 0:rows, :] = key_part.astype(BF16)
@@ -305,17 +303,15 @@
             def _():
                 send_parts(o)
 
-        u = i - 1 + side
-
-        @pl.when(lax.rem(u, 2) == 0)
-        def _():
-            @pl.when((u >= 2) & (reach - u <= here))
-            def _():
-                join_twin(reach - u)
-
-            @pl.when((u >= 4) & (reach + 2 - u <= here))
-            def _():
-                send_back(reach + 2 - u)
+        @pl.when(lax.rem(i, 2) == 0)
+        def _():
+            @pl.when((i >= 2) & (reach - i <= here))
+            def _():
+                join_twin(reach - i)
+
+            @pl.when((i >= 4) & (reach + 2 - i <= here))
+            def _():
+                send_back(reach + 2 - i)
 
         @pl.when((side == 0) & (i == 2) & (here >= last))
         def _():
@@ -324,11 +320,12 @@
         return 0
 
     lax.fori_loop(0, reach, grad_step, 0)
-    join_twin(0)
 
     @pl.when(here >= 2)
     def _():
         send_back(2)
+
+    join_twin(0)
 
     for h in range(heads):
         block = dqt[:, h * rows:(h + 1) * rows] * scale
@@ -377,13 +374,9 @@
 
 
 def finish(*refs):
-    count = (len(refs) - 1) // 2
-    sems = refs[-1]
-    copies = [pltpu.make_async_copy(refs[i], refs[count + i], sems.at[i]) for i in range(count)]
-    for copy in copies:
-        copy.start()
-    for copy in copies:
-        copy.wait()
+    count = len(refs) // 2
+    for i in range(count):
+        refs[count + i][...] = refs[i][...]
 
 
 def local(n, parts, queries, keys, values, grad_out, doc_of_block, pair_list, knock):
@@ -409,6 +402,10 @@
             pltpu.VMEM((reach, 2 * rows, width), BF16),
             pltpu.VMEM((width, heads * rows), BF16),
             pltpu.VMEM((width, heads * rows), BF16),
+            pltpu.VMEM((heads * rows, width), BF16),
+            pltpu.VMEM((heads * rows, width), BF16),
+            pltpu.VMEM((rows, heads * rows), BF16),
+            pltpu.VMEM((rows, heads * rows), BF16),
             pltpu.VMEM((reach, rows, heads * rows), F32),
             pltpu.VMEM((reach, rows, heads * rows), F32),
             pltpu.VMEM((reach, heads, rows), F32),
@@ -436,14 +433,11 @@
         cost_estimate=pl.CostEstimate(
             flops=10 * tiles * width, bytes_accessed=4 * 2 * rows * heads * width, transcendentals=tiles),
     )(queries, keys, values, grad_out, doc_of_block, pair_list, knock)
-    anywhere = pl.BlockSpec(memory_space=pl.ANY)
     return pl.pallas_call(
         finish,
         out_shape=tuple(jax.ShapeDtypeStruct(x.shape, x.dtype) for x in results),
-        in_specs=[anywhere] * 3,
-        out_specs=(anywhere,) * 3,
-        scratch_shapes=[dma((3,))],
-        compiler_params=pltpu.CompilerParams(vmem_limit_bytes=56 * 1024 * 1024),
+        in_specs=[vmem] * 3,
+        out_specs=(vmem,) * 3,
     )(*results)
 
 

time: 67.2 us -> 46.9 us (0.70)
  Pallas kernels: 65.9 us -> 46.1 us
    pallas_call x1, Pallas kernels: 21 us -> 1.92 us  [local(): pl.pallas_call(finish, out_shape=tuple((jax.ShapeDtypeStruct(x.shape, x.d...]
    pallas_call x1, Pallas kernels: 44.9 us -> 44.2 us  [local(): pl.pallas_call(functools.partial(kernel, n, parts, reach, heads, rows, wi...]
where the time goes in v3:
time: 46.9 us; the launch traced here: 46.7 us
  Pallas kernels  46.1 us (98%)
  between operations  0.64 us (1%)
    pallas_call x1, Pallas kernels, local(): pl.pallas_call(functools.partial(kernel, n, parts, reach, heads, rows, wi...  44.2 us
    pallas_call x1, Pallas kernels, local(): pl.pallas_call(finish, out_shape=tuple((jax.ShapeDtypeStruct(x.shape, x.d...  1.92 us

profile of v3, /device:TPU:12, one launch (start us, length us, event | category | flops | bytes accessed | tf_op | source)
XLA Modules:
  0.0 46.7 jit_solution(4867081759178405112)
XLA Ops:
  0.6 44.2 %shard_map.94 = (bf16[256,1024]{1,0:T(8,128)(2,1)}, bf16[256,128]{1,0:T(8,128)(2,1)}, bf16[256,128]{1,0:T(8,128)(2,1)}) custom-call(bf16[256,1024]{1,0:T(8,128)(2,1)} %q.1, bf16[256,128]{1,0:T(8,128)(2,1)} %k.1, bf16[256,128]{1,0:T(8,128)(2,1)} %v.1, bf16[256,1024]{1,0:T(8,128)(2,1)} %g.1, s32[16]{0:T(128)} %doc.1, s32[1,7]{1,0:T(1,128)} %pair.1, s32[8,16]{1,0:T(8,128)} %knock.1), custom_call_target="tpu_custom_call" | custom-call | flops 5368709120 | bytes 2097152 | tf_op jit(solution)/shard_map/pallas_call | solution.py:392
  44.8 1.9 %shard_map.95 = (bf16[256,1024]{1,0:T(8,128)(2,1)}, bf16[256,128]{1,0:T(8,128)(2,1)}, bf16[256,128]{1,0:T(8,128)(2,1)}) custom-call(bf16[256,1024]{1,0:T(8,128)(2,1)} %get-tuple-element.6.refs_0_, bf16[256,128]{1,0:T(8,128)(2,1)} %get-tuple-element.7.refs_1_, bf16[256,128]{1,0:T(8,128)(2,1)} %get-tuple-element.8.refs_2_), custom_call_target="tpu_custom_call" | custom-call | tf_op jit(solution)/shard_map/pallas_call | solution.py:436

commit v4 on v3

--- a/solution.py
+++ b/solution.py
@@ -179,21 +179,32 @@
             for j in range(reach - 1):
                 listed = listed + (pair[0, j] == o).astype(jnp.int32)
             allowed = jnp.minimum(listed, 1) * (doc[source] == doc[here]).astype(jnp.int32)
-        for h in range(heads):
+
+        def products(h):
             cols = slice(h * rows, (h + 1) * rows)
             raw = jnp.dot(keys, qt[:, cols], preferred_element_type=F32)
-            grad_probs = jnp.dot(values, gt[:, cols], preferred_element_type=F32)
             if own:
                 raw = jnp.where(lower, raw, NEG)
-                now = jnp.max(raw, axis=0, keepdims=True) * coef
+            e_s[o, :, cols] = raw
+            dp_s[o, :, cols] = jnp.dot(values, gt[:, cols], preferred_element_type=F32)
+            return jnp.max(raw, axis=0, keepdims=True) * coef
+
+        highest = [products(0)]
+        for h in range(heads):
+            if h + 1 < heads:
+                highest.append(products(h + 1))
+            cols = slice(h * rows, (h + 1) * rows)
+            raw = e_s[o, :, cols]
+            grad_probs = dp_s[o, :, cols]
+            if own:
+                now = highest[h]
                 shifted = jnp.exp2(raw * coef - now)
                 total[h:h + 1, :] = jnp.sum(shifted, axis=0, keepdims=True)
                 weighted[h:h + 1, :] = jnp.sum(shifted * grad_probs, axis=0, keepdims=True)
             else:
                 live = jnp.full((1, rows), allowed * knock[h, source], jnp.int32) == 1
                 before = top[h:h + 1, :]
-                now = jnp.where(
-                    live, jnp.maximum(before, jnp.max(raw, axis=0, keepdims=True) * coef), before)
+                now = jnp.where(live, jnp.maximum(before, highest[h]), before)
                 factor = jnp.exp2(before - now)
                 shifted = jnp.exp2(raw * coef - jnp.where(live, now, BIG))
                 total[h:h + 1, :] = total[h:h + 1, :] * factor + jnp.sum(shifted, axis=0, keepdims=True)
@@ -202,7 +213,6 @@
             top[h:h + 1, :] = now
             tops[o, h:h + 1, :] = now
             e_s[o, :, cols] = shifted
-            dp_s[o, :, cols] = grad_probs
 
     def slot_at(t):
         inner = jnp.where(lax.rem(t, 2) == 1, t + 1, jnp.maximum(t - 1, 0))

time: 46.9 us -> 47 us (level)
  no operation moved by 1% of the time
where the time goes in v4:
time: 47 us; the launch traced here: 46.9 us
  Pallas kernels  46.2 us (98%)
  between operations  0.64 us (1%)
    pallas_call x1, Pallas kernels, local(): pl.pallas_call(functools.partial(kernel, n, parts, reach, heads, rows, wi...  44.3 us
    pallas_call x1, Pallas kernels, local(): pl.pallas_call(finish, out_shape=tuple((jax.ShapeDtypeStruct(x.shape, x.d...  1.92 us

profile of v4, /device:TPU:12, one launch (start us, length us, event | category | flops | bytes accessed | tf_op | source)
XLA Modules:
  0.0 46.9 jit_solution(9613895999857715265)
XLA Ops:
  0.6 44.3 %shard_map.94 = (bf16[256,1024]{1,0:T(8,128)(2,1)}, bf16[256,128]{1,0:T(8,128)(2,1)}, bf16[256,128]{1,0:T(8,128)(2,1)}) custom-call(bf16[256,1024]{1,0:T(8,128)(2,1)} %q.1, bf16[256,128]{1,0:T(8,128)(2,1)} %k.1, bf16[256,128]{1,0:T(8,128)(2,1)} %v.1, bf16[256,1024]{1,0:T(8,128)(2,1)} %g.1, s32[16]{0:T(128)} %doc.1, s32[1,7]{1,0:T(1,128)} %pair.1, s32[8,16]{1,0:T(8,128)} %knock.1), custom_call_target="tpu_custom_call" | custom-call | flops 5368709120 | bytes 2097152 | tf_op jit(solution)/shard_map/pallas_call | solution.py:402
  44.9 1.9 %shard_map.95 = (bf16[256,1024]{1,0:T(8,128)(2,1)}, bf16[256,128]{1,0:T(8,128)(2,1)}, bf16[256,128]{1,0:T(8,128)(2,1)}) custom-call(bf16[256,1024]{1,0:T(8,128)(2,1)} %get-tuple-element.6.refs_0_, bf16[256,128]{1,0:T(8,128)(2,1)} %get-tuple-element.7.refs_1_, bf16[256,128]{1,0:T(8,128)(2,1)} %get-tuple-element.8.refs_2_), custom_call_target="tpu_custom_call" | custom-call | tf_op jit(solution)/shard_map/pallas_call | solution.py:446

commit v5 on v4

--- a/solution.py
+++ b/solution.py
@@ -21,8 +21,9 @@
 
 def kernel(
     n, parts, reach, heads, rows, width,
-    q, k, v, g, doc, pair, knock,
-    dq, dk, dv,
+    q_hbm, k, v, g_hbm, doc, pair, knock,
+    dq_hbm, dk, dv,
+    q, g, dq, local_sem,
     kv, qt, gt, qs, gs, p_low, g_low, e_s, dp_s, tops, top, total, weighted, dqt,
     pf, part, sx, rx, red, rc, fin,
     gather_send, gather_recv, pass_send, pass_recv, twin_send, twin_recv,
@@ -117,6 +118,12 @@
     ahead = [(r, here + r < n) for r in evens] + [(last, (here + last < n) & (side == 1))]
     behind = [(r, here >= r) for r in evens] + [(last, (here >= last) & (side == 0))]
 
+    load_q = pltpu.make_async_copy(q_hbm, q, local_sem.at[0])
+    load_g = pltpu.make_async_copy(g_hbm, g, local_sem.at[1])
+    store_dq = pltpu.make_async_copy(dq, dq_hbm, local_sem.at[2])
+    load_q.start()
+    load_g.start()
+
     barrier = pltpu.get_barrier_semaphore()
     greeted = jnp.int32(parts)
     for r, there in ahead:
@@ -149,6 +156,8 @@
     def _():
         twin_copy(0).start()
 
+    load_q.wait()
+    load_g.wait()
     for h in range(heads):
         qt[:, h * rows:(h + 1) * rows] = transposed(q[:, h * width:(h + 1) * width])
         gt[:, h * rows:(h + 1) * rows] = transposed(g[:, h * width:(h + 1) * width])
@@ -341,6 +350,7 @@
         block = dqt[:, h * rows:(h + 1) * rows] * scale
         dq[:, h * width:(h + 1) * width] = block.T.astype(BF16)
 
+    store_dq.start()
     pf[0, my_rows, :] = head_sum(0)
     for r, there in reversed(ahead):
         @pl.when(there)
@@ -356,6 +366,7 @@
     dk[...] = fin[0:rows, :]
     dv[...] = fin[rows:2 * rows, :]
 
+    store_dq.wait()
     for r, there in ahead:
         @pl.when(there)
         def _():
@@ -396,6 +407,7 @@
     share = 2 * rows // parts
     others = parts - 1
     vmem = pl.BlockSpec(memory_space=pltpu.VMEM)
+    anywhere = pl.BlockSpec(memory_space=pl.ANY)
     smem = pl.BlockSpec(memory_space=pltpu.SMEM)
     dma = pltpu.SemaphoreType.DMA
     tiles = reach * heads * rows * rows
@@ -406,9 +418,13 @@
             jax.ShapeDtypeStruct(keys.shape, BF16),
             jax.ShapeDtypeStruct(values.shape, BF16),
         ),
-        in_specs=[vmem] * 4 + [smem] * 3,
-        out_specs=(vmem,) * 3,
+        in_specs=[anywhere, vmem, vmem, anywhere] + [smem] * 3,
+        out_specs=(anywhere, vmem, vmem),
         scratch_shapes=[
+            pltpu.VMEM(queries.shape, BF16),
+            pltpu.VMEM(queries.shape, BF16),
+            pltpu.VMEM(queries.shape, BF16),
+            dma((3,)),
             pltpu.VMEM((reach, 2 * rows, width), BF16),
             pltpu.VMEM((width, heads * rows), BF16),
             pltpu.VMEM((width, heads * rows), BF16),

time: 47 us -> 46.5 us (0.989)
  Pallas kernels: 46.2 us -> 45.7 us
    pallas_call x1, Pallas kernels: 44.3 us -> 43.7 us  [local(): pl.pallas_call(functools.partial(kernel, n, parts, reach, heads, rows, wi...]
where the time goes in v5:
time: 46.5 us; the launch traced here: 46.3 us
  Pallas kernels  45.7 us (98%)
  between operations  0.64 us (1%)
    pallas_call x1, Pallas kernels, local(): pl.pallas_call(functools.partial(kernel, n, parts, reach, heads, rows, wi...  43.7 us
    pallas_call x1, Pallas kernels, local(): pl.pallas_call(finish, out_shape=tuple((jax.ShapeDtypeStruct(x.shape, x.d...  1.92 us

profile of v5, /device:TPU:12, one launch (start us, length us, event | category | flops | bytes accessed | tf_op | source)
XLA Modules:
  0.0 46.3 jit_solution(10493228969236085301)
XLA Ops:
  0.6 43.7 %shard_map.94 = (bf16[256,1024]{1,0:T(8,128)(2,1)}, bf16[256,128]{1,0:T(8,128)(2,1)}, bf16[256,128]{1,0:T(8,128)(2,1)}) custom-call(bf16[256,1024]{1,0:T(8,128)(2,1)} %q_hbm.1, bf16[256,128]{1,0:T(8,128)(2,1)} %k.1, bf16[256,128]{1,0:T(8,128)(2,1)} %v.1, bf16[256,1024]{1,0:T(8,128)(2,1)} %g_hbm.1, s32[16]{0:T(128)} %doc.1, s32[1,7]{1,0:T(1,128)} %pair.1, ...), custom_call_target="tpu_custom_call" | custom-call | flops 5368709120 | bytes 2097152 | tf_op jit(solution)/shard_map/pallas_call | solution.py:414
  44.4 1.9 %shard_map.95 = (bf16[256,1024]{1,0:T(8,128)(2,1)}, bf16[256,128]{1,0:T(8,128)(2,1)}, bf16[256,128]{1,0:T(8,128)(2,1)}) custom-call(bf16[256,1024]{1,0:T(8,128)(2,1)} %get-tuple-element.6.refs_0_, bf16[256,128]{1,0:T(8,128)(2,1)} %get-tuple-element.7.refs_1_, bf16[256,128]{1,0:T(8,128)(2,1)} %get-tuple-element.8.refs_2_), custom_call_target="tpu_custom_call" | custom-call | tf_op jit(solution)/shard_map/pallas_call | solution.py:462
